TPU v7x, 1024 devices: a whole 4x4x32 slice. The times are simulated.
1024 devices in a mesh: dp: 128 (over x_lo, z, core), group: 8 (over x_hi, y).
Axes of the slice: x: 4 (x_hi: 2, x_lo: 2; x = x_hi * 2 + x_lo), y: 4, z: 32, core: 2. Of those that a mesh axis runs over, the one named last changes fastest.
Arguments:
- picture_vectors: bfloat16 [8, 16384, 1152], P('group', 'dp'), may hold values from -6 to 6
- caption_vectors: bfloat16 [8, 16384, 1152], P('group', 'dp'), may hold values from -6 to 6
- matched_caption_slot: int32 [8, 128, 128], P('group', 'dp'), may hold values from 0 to 127, each once within a row
- sharpness_coefficient: float32 [1], replicated, may hold values from 2 to 8
- affinity_offset: float32 [1], replicated, may hold values from -3 to -1
Outputs:
- picture_derivative: float32 [8, 16384, 1152], P('group', 'dp')
- text_grad: float32 [8, 16384, 1152], P('group', 'dp')
Inputs may be any that keep to these rules, and one draw needn't show every extreme that they name: `matched_caption_slot`: each row of one device is a permutation of 0 .. 127.
All inputs are finite; a program needn't handle non-finite values.
Results may differ from a plain program's by a relative error of at most 0.0085.
Values may be sent and summed in bfloat16 or wider, within the bound.
No kernel may reach another device: no remote copies, remote signals or barrier semaphores. Data moves between devices by JAX's collectives and lax.ppermute only.
A program may use at most 32 MiB of HBM per device.

v0:
```python
import jax
import jax.numpy as jnp
from jax import lax
from jax.sharding import PartitionSpec as P

ROUNDS = 8


def swapped(block, axis, apart):
    count = lax.axis_size(axis)
    route = []
    for low in range(count):
        high = low | 1 << apart
        if high != low and high < count:
            route += [(low, high), (high, low)]
    return lax.ppermute(block, axis, route)


def normalize(values):
    wide = values.astype(jnp.float32)
    inverse_norm_factor = lax.rsqrt(jnp.sum(wide * wide, axis=-1, keepdims=True) + 1e-06)
    return (wide * inverse_norm_factor, inverse_norm_factor)


def fetch_block(block, lower_bits_mask, high_mask):
    for bit_pos in range(2):
        if lower_bits_mask >> bit_pos & 1:
            block = swapped(block, "dp", bit_pos)
    if high_mask:
        block = swapped(block, "group", 0)
    return block


def return_part(piece, lower_bits_mask, high_mask):
    for bit_pos in range(2):
        if lower_bits_mask >> bit_pos & 1:
            piece = swapped(piece, "dp", bit_pos)
    if high_mask:
        piece = swapped(piece, "group", 0)
    return piece


def on_device(
    picture_vectors, caption_vectors, matched_caption_slot, sharpness_coefficient, affinity_offset
):
    xn, inv_x = normalize(picture_vectors[0])
    yn, inv_y = normalize(caption_vectors[0])
    image_half_rows = xn.astype(jnp.bfloat16)
    y_half = yn.astype(jnp.bfloat16)
    similarity_multiplier = sharpness_coefficient[0]
    shift = affinity_offset[0]
    count = image_half_rows.shape[0]
    columns = lax.broadcasted_iota(jnp.int32, (count, count), 1)
    positive = matched_caption_slot[0, 0][:, None] == columns
    image_embedding_gradient = jnp.zeros(xn.shape, jnp.float32)
    grad_y = jnp.zeros(yn.shape, jnp.float32)
    for step in range(ROUNDS):
        lower_bits_mask = step % 4
        high_mask = step // 4
        block = fetch_block(y_half, lower_bits_mask, high_mask)
        logits = (
            similarity_multiplier
            * jnp.dot(image_half_rows, block.T, preferred_element_type=jnp.float32)
            + shift
        )
        if step == 0:
            sign = jnp.where(positive, 1.0, -1.0).astype(jnp.float32)
        else:
            sign = -jnp.ones_like(logits)
        coef = (-similarity_multiplier * sign * jax.nn.sigmoid(-sign * logits)).astype(jnp.bfloat16)
        image_term = jnp.dot(coef, block, preferred_element_type=jnp.float32)
        caption_contribution = lax.dot_general(
            coef, image_half_rows, (((0,), (0,)), ((), ())), preferred_element_type=jnp.float32
        )
        image_term, caption_contribution = (image_term, caption_contribution.astype(jnp.bfloat16))
        image_embedding_gradient = image_embedding_gradient + image_term
        grad_y = grad_y + return_part(caption_contribution, lower_bits_mask, high_mask).astype(
            jnp.float32
        )
    picture_derivative = (
        image_embedding_gradient
        - xn * jnp.sum(xn * image_embedding_gradient, axis=-1, keepdims=True)
    ) * inv_x
    text_grad = (grad_y - yn * jnp.sum(yn * grad_y, axis=-1, keepdims=True)) * inv_y
    return (picture_derivative[None], text_grad[None])


def solution(mesh):
    in_specs = (P("group", "dp", None), P("group", "dp", None), P("group", "dp", None), P(), P())
    out_specs = (P("group", "dp", None), P("group", "dp", None))
    return jax.shard_map(
        on_device, mesh=mesh, in_specs=in_specs, out_specs=out_specs, check_vma=False
    )
```

profile of v0, /device:TPU:1, one launch (start us, length us, event | category | flops | bytes accessed | tf_op | source)
XLA Modules:
  0.0 100.6 jit_solution(17920917821458440208)
XLA Ops:
  2.0 4.4 %collective-permute-start.1 = (bf16[128,1152]{1,0:T(8,128)(2,1)S(1)}, bf16[128,1152]{1,0:T(8,128)(2,1)S(1)}, u32[]{:S(2)}, u32[]{:S(2)}) collective-permute-start(bf16[128,1152]{1,0:T(8,128)(2,1)S(1)} %fusion.64), channel_id=1, source_target_pairs={{0,16},{16,0},{8,24},{24,8},{32,48},{48,32},{40,56},{56,40},{64,80... | collective-permute-start | bytes 884744 | tf_op jit(solution)/shard_map/ppermute | solution.py:16
  6.3 3.2 %collective-permute-start.3 = (bf16[128,1152]{1,0:T(8,128)(2,1)S(1)}, bf16[128,1152]{1,0:T(8,128)(2,1)S(1)}, u32[]{:S(2)}, u32[]{:S(2)}) collective-permute-start(bf16[128,1152]{1,0:T(8,128)(2,1)S(1)} %fusion.64), channel_id=1, source_target_pairs={{0,1},{1,0},{2,3},{3,2},{4,5},{5,4},{6,7},{7,6},{8,9},{9,8},{10,11... | collective-permute-start | bytes 884744 | tf_op jit(solution)/shard_map/ppermute | solution.py:16
  9.6 12.3 %collective-permute-start = (bf16[128,1152]{1,0:T(8,128)(2,1)S(1)}, bf16[128,1152]{1,0:T(8,128)(2,1)S(1)}, u32[]{:S(2)}, u32[]{:S(2)}) collective-permute-start(bf16[128,1152]{1,0:T(8,128)(2,1)S(1)} %fusion.64), channel_id=1, source_target_pairs={{0,8},{8,0},{16,24},{24,16},{32,40},{40,32},{48,56},{56,48},{64,72... | collective-permute-start | bytes 884744 | tf_op jit(solution)/shard_map/ppermute | solution.py:16
  25.5 3.6 %collective-permute-start.11 = (bf16[128,1152]{1,0:T(8,128)(2,1)S(1)}, bf16[128,1152]{1,0:T(8,128)(2,1)S(1)}, u32[]{:S(2)}, u32[]{:S(2)}) collective-permute-start(bf16[128,1152]{1,0:T(8,128)(2,1)S(1)} %convolution_convert_fusion.3), channel_id=1, source_target_pairs={{0,1},{1,0},{2,3},{3,2},{4,5},{5,4},{6,7},{7,6},{8,9},{9,8},{10,11... | collective-permute-start | bytes 884744 | tf_op jit(solution)/shard_map/ppermute | solution.py:16
  29.8 3.6 %collective-permute-start.8 = (bf16[128,1152]{1,0:T(8,128)(2,1)S(1)}, bf16[128,1152]{1,0:T(8,128)(2,1)S(1)}, u32[]{:S(2)}, u32[]{:S(2)}) collective-permute-start(bf16[128,1152]{1,0:T(8,128)(2,1)S(1)} %convolution_convert_fusion.5), channel_id=1, source_target_pairs={{0,16},{16,0},{8,24},{24,8},{32,48},{48,32},{40,56},{56,40},{64,80... | collective-permute-start | bytes 884744 | tf_op jit(solution)/shard_map/ppermute | solution.py:16
  34.1 1.9 %collective-permute-start.5 = (bf16[128,1152]{1,0:T(8,128)(2,1)S(1)}, bf16[128,1152]{1,0:T(8,128)(2,1)S(1)}, u32[]{:S(2)}, u32[]{:S(2)}) collective-permute-start(bf16[128,1152]{1,0:T(8,128)(2,1)S(1)} %collective-permute-done.1), channel_id=1, source_target_pairs={{0,1},{1,0},{2,3},{3,2},{4,5},{5,4},{6,7},{7,6},{8,9},{9,8},{10,11... | collective-permute-start | bytes 884744 | tf_op jit(solution)/shard_map/ppermute | solution.py:16
  36.3 1.9 %collective-permute-start.2 = (bf16[128,1152]{1,0:T(8,128)(2,1)S(1)}, bf16[128,1152]{1,0:T(8,128)(2,1)S(1)}, u32[]{:S(2)}, u32[]{:S(2)}) collective-permute-start(bf16[128,1152]{1,0:T(8,128)(2,1)S(1)} %collective-permute-done), channel_id=1, source_target_pairs={{0,16},{16,0},{8,24},{24,8},{32,48},{48,32},{40,56},{56,40},{64,80... | collective-permute-start | bytes 884744 | tf_op jit(solution)/shard_map/ppermute | solution.py:16
  38.2 3.4 %collective-permute-start.4 = (bf16[128,1152]{1,0:T(8,128)(2,1)S(1)}, bf16[128,1152]{1,0:T(8,128)(2,1)S(1)}, u32[]{:S(2)}, u32[]{:S(2)}) collective-permute-start(bf16[128,1152]{1,0:T(8,128)(2,1)S(1)} %collective-permute-done), channel_id=1, source_target_pairs={{0,1},{1,0},{2,3},{3,2},{4,5},{5,4},{6,7},{7,6},{8,9},{9,8},{10,11... | collective-permute-start | bytes 884744 | tf_op jit(solution)/shard_map/ppermute | solution.py:16
  42.1 2.0 %collective-permute-done.5 = bf16[128,1152]{1,0:T(8,128)(2,1)S(1)} collective-permute-done((bf16[128,1152]{1,0:T(8,128)(2,1)S(1)}, bf16[128,1152]{1,0:T(8,128)(2,1)S(1)}, u32[]{:S(2)}, u32[]{:S(2)}) %collective-permute-start.5) | collective-permute-done | bytes 294944 | tf_op jit(solution)/shard_map/ppermute | solution.py:16
  44.7 2.2 %collective-permute-start.14 = (bf16[128,1152]{1,0:T(8,128)(2,1)S(1)}, bf16[128,1152]{1,0:T(8,128)(2,1)S(1)}, u32[]{:S(2)}, u32[]{:S(2)}) collective-permute-start(bf16[128,1152]{1,0:T(8,128)(2,1)S(1)} %convolution_convert_fusion.1), channel_id=1, source_target_pairs={{0,16},{16,0},{8,24},{24,8},{32,48},{48,32},{40,56},{56,40},{64,80... | collective-permute-start | bytes 884744 | tf_op jit(solution)/shard_map/ppermute | solution.py:16
  46.9 3.5 %collective-permute-done.4 = bf16[128,1152]{1,0:T(8,128)(2,1)S(1)} collective-permute-done((bf16[128,1152]{1,0:T(8,128)(2,1)S(1)}, bf16[128,1152]{1,0:T(8,128)(2,1)S(1)}, u32[]{:S(2)}, u32[]{:S(2)}) %collective-permute-start.4) | collective-permute-done | bytes 294944 | tf_op jit(solution)/shard_map/ppermute | solution.py:16
  51.0 3.3 %collective-permute-start.12 = (bf16[128,1152]{1,0:T(8,128)(2,1)S(1)}, bf16[128,1152]{1,0:T(8,128)(2,1)S(1)}, u32[]{:S(2)}, u32[]{:S(2)}) collective-permute-start(bf16[128,1152]{1,0:T(8,128)(2,1)S(1)} %convolution_convert_fusion.2), channel_id=1, source_target_pairs={{0,8},{8,0},{16,24},{24,16},{32,40},{40,32},{48,56},{56,48},{64,72... | collective-permute-start | bytes 884744 | tf_op jit(solution)/shard_map/ppermute | solution.py:16
  54.3 1.9 %collective-permute-start.6 = (bf16[128,1152]{1,0:T(8,128)(2,1)S(1)}, bf16[128,1152]{1,0:T(8,128)(2,1)S(1)}, u32[]{:S(2)}, u32[]{:S(2)}) collective-permute-start(bf16[128,1152]{1,0:T(8,128)(2,1)S(1)} %collective-permute-done.2), channel_id=1, source_target_pairs={{0,1},{1,0},{2,3},{3,2},{4,5},{5,4},{6,7},{7,6},{8,9},{9,8},{10,11... | collective-permute-start | bytes 884744 | tf_op jit(solution)/shard_map/ppermute | solution.py:16
  56.8 8.0 %collective-permute-done.6 = bf16[128,1152]{1,0:T(8,128)(2,1)S(1)} collective-permute-done((bf16[128,1152]{1,0:T(8,128)(2,1)S(1)}, bf16[128,1152]{1,0:T(8,128)(2,1)S(1)}, u32[]{:S(2)}, u32[]{:S(2)}) %collective-permute-start.6) | collective-permute-done | bytes 294944 | tf_op jit(solution)/shard_map/ppermute | solution.py:16
  65.5 2.7 %collective-permute-start.16 = (bf16[128,1152]{1,0:T(8,128)(2,1)S(1)}, bf16[128,1152]{1,0:T(8,128)(2,1)S(1)}, u32[]{:S(2)}, u32[]{:S(2)}) collective-permute-start(bf16[128,1152]{1,0:T(8,128)(2,1)S(1)} %convolution_convert_fusion), channel_id=1, source_target_pairs={{0,8},{8,0},{16,24},{24,16},{32,40},{40,32},{48,56},{56,48},{64,72... | collective-permute-start | bytes 884744 | tf_op jit(solution)/shard_map/ppermute | solution.py:16
  68.8 1.9 %collective-permute-start.9 = (bf16[128,1152]{1,0:T(8,128)(2,1)S(1)}, bf16[128,1152]{1,0:T(8,128)(2,1)S(1)}, u32[]{:S(2)}, u32[]{:S(2)}) collective-permute-start(bf16[128,1152]{1,0:T(8,128)(2,1)S(1)} %convolution_convert_fusion.4), channel_id=1, source_target_pairs={{0,8},{8,0},{16,24},{24,16},{32,40},{40,32},{48,56},{56,48},{64,72... | collective-permute-start | bytes 884744 | tf_op jit(solution)/shard_map/ppermute | solution.py:16
  70.7 1.9 %collective-permute-start.17 = (bf16[128,1152]{1,0:T(8,128)(2,1)S(1)}, bf16[128,1152]{1,0:T(8,128)(2,1)S(1)}, u32[]{:S(2)}, u32[]{:S(2)}) collective-permute-start(bf16[128,1152]{1,0:T(8,128)(2,1)S(1)} %collective-permute-done.16), channel_id=1, source_target_pairs={{0,16},{16,0},{8,24},{24,8},{32,48},{48,32},{40,56},{56,40},{64,80... | collective-permute-start | bytes 884744 | tf_op jit(solution)/shard_map/ppermute | solution.py:16
  73.2 2.7 %collective-permute-start.7 = (bf16[128,1152]{1,0:T(8,128)(2,1)S(1)}, bf16[128,1152]{1,0:T(8,128)(2,1)S(1)}, u32[]{:S(2)}, u32[]{:S(2)}) collective-permute-start(bf16[128,1152]{1,0:T(8,128)(2,1)S(1)} %convolution_convert_fusion.6), channel_id=1, source_target_pairs={{0,8},{8,0},{16,24},{24,16},{32,40},{40,32},{48,56},{56,48},{64,72... | collective-permute-start | bytes 884744 | tf_op jit(solution)/shard_map/ppermute | solution.py:16
  75.9 3.1 %collective-permute-start.15 = (bf16[128,1152]{1,0:T(8,128)(2,1)S(1)}, bf16[128,1152]{1,0:T(8,128)(2,1)S(1)}, u32[]{:S(2)}, u32[]{:S(2)}) collective-permute-start(bf16[128,1152]{1,0:T(8,128)(2,1)S(1)} %collective-permute-done.14), channel_id=1, source_target_pairs={{0,1},{1,0},{2,3},{3,2},{4,5},{5,4},{6,7},{7,6},{8,9},{9,8},{10,11... | collective-permute-start | bytes 884744 | tf_op jit(solution)/shard_map/ppermute | solution.py:16
  79.0 2.2 %collective-permute-start.13 = (bf16[128,1152]{1,0:T(8,128)(2,1)S(1)}, bf16[128,1152]{1,0:T(8,128)(2,1)S(1)}, u32[]{:S(2)}, u32[]{:S(2)}) collective-permute-start(bf16[128,1152]{1,0:T(8,128)(2,1)S(1)} %collective-permute-done.12), channel_id=1, source_target_pairs={{0,1},{1,0},{2,3},{3,2},{4,5},{5,4},{6,7},{7,6},{8,9},{9,8},{10,11... | collective-permute-start | bytes 884744 | tf_op jit(solution)/shard_map/ppermute | solution.py:16
  81.2 3.4 %collective-permute-start.10 = (bf16[128,1152]{1,0:T(8,128)(2,1)S(1)}, bf16[128,1152]{1,0:T(8,128)(2,1)S(1)}, u32[]{:S(2)}, u32[]{:S(2)}) collective-permute-start(bf16[128,1152]{1,0:T(8,128)(2,1)S(1)} %collective-permute-done.9), channel_id=1, source_target_pairs={{0,16},{16,0},{8,24},{24,8},{32,48},{48,32},{40,56},{56,40},{64,80... | collective-permute-start | bytes 884744 | tf_op jit(solution)/shard_map/ppermute | solution.py:16
  84.6 1.9 %collective-permute-start.18 = (bf16[128,1152]{1,0:T(8,128)(2,1)S(1)}, bf16[128,1152]{1,0:T(8,128)(2,1)S(1)}, u32[]{:S(2)}, u32[]{:S(2)}) collective-permute-start(bf16[128,1152]{1,0:T(8,128)(2,1)S(1)} %collective-permute-done.17), channel_id=1, source_target_pairs={{0,1},{1,0},{2,3},{3,2},{4,5},{5,4},{6,7},{7,6},{8,9},{9,8},{10,11... | collective-permute-start | bytes 884744 | tf_op jit(solution)/shard_map/ppermute | solution.py:16
  87.6 5.2 %collective-permute-done.13 = bf16[128,1152]{1,0:T(8,128)(2,1)S(1)} collective-permute-done((bf16[128,1152]{1,0:T(8,128)(2,1)S(1)}, bf16[128,1152]{1,0:T(8,128)(2,1)S(1)}, u32[]{:S(2)}, u32[]{:S(2)}) %collective-permute-start.13) | collective-permute-done | bytes 294944 | tf_op jit(solution)/shard_map/ppermute | solution.py:16
  92.8 6.3 %collective-permute-done.18 = bf16[128,1152]{1,0:T(8,128)(2,1)S(1)} collective-permute-done((bf16[128,1152]{1,0:T(8,128)(2,1)S(1)}, bf16[128,1152]{1,0:T(8,128)(2,1)S(1)}, u32[]{:S(2)}, u32[]{:S(2)}) %collective-permute-start.18) | collective-permute-done | bytes 294944 | tf_op jit(solution)/shard_map/ppermute | solution.py:16
  (52 shorter events, 11.6 us)
Async XLA Ops:
  0.6 1.2 %copy-start.1 = (bf16[1,128,1152]{2,1,0:T(8,128)(2,1)S(1)}, bf16[1,128,1152]{2,1,0:T(8,128)(2,1)}, u32[]{:S(2)}) copy-start(bf16[1,128,1152]{2,1,0:T(8,128)(2,1)} %param.6) | copy-start | bytes 884740
  1.8 20.1 %copy-start = (bf16[1,128,1152]{2,1,0:T(8,128)(2,1)S(1)}, bf16[1,128,1152]{2,1,0:T(8,128)(2,1)}, u32[]{:S(2)}) copy-start(bf16[1,128,1152]{2,1,0:T(8,128)(2,1)} %param.5) | copy-start | bytes 884740
  2.0 27.2 %collective-permute-start.1 = (bf16[128,1152]{1,0:T(8,128)(2,1)S(1)}, bf16[128,1152]{1,0:T(8,128)(2,1)S(1)}, u32[]{:S(2)}, u32[]{:S(2)}) collective-permute-start(bf16[128,1152]{1,0:T(8,128)(2,1)S(1)} %fusion.64), channel_id=1, source_target_pairs={{0,16},{16,0},{8,24},{24,8},{32,48},{48,32},{40,56},{56,40},{64,80... | collective-permute-start | bytes 884744 | tf_op jit(solution)/shard_map/ppermute | solution.py:16
  6.3 18.6 %collective-permute-start.3 = (bf16[128,1152]{1,0:T(8,128)(2,1)S(1)}, bf16[128,1152]{1,0:T(8,128)(2,1)S(1)}, u32[]{:S(2)}, u32[]{:S(2)}) collective-permute-start(bf16[128,1152]{1,0:T(8,128)(2,1)S(1)} %fusion.64), channel_id=1, source_target_pairs={{0,1},{1,0},{2,3},{3,2},{4,5},{5,4},{6,7},{7,6},{8,9},{9,8},{10,11... | collective-permute-start | bytes 884744 | tf_op jit(solution)/shard_map/ppermute | solution.py:16
  9.6 23.9 %collective-permute-start = (bf16[128,1152]{1,0:T(8,128)(2,1)S(1)}, bf16[128,1152]{1,0:T(8,128)(2,1)S(1)}, u32[]{:S(2)}, u32[]{:S(2)}) collective-permute-start(bf16[128,1152]{1,0:T(8,128)(2,1)S(1)} %fusion.64), channel_id=1, source_target_pairs={{0,8},{8,0},{16,24},{24,16},{32,40},{40,32},{48,56},{56,48},{64,72... | collective-permute-start | bytes 884744 | tf_op jit(solution)/shard_map/ppermute | solution.py:16
  23.3 0.7 copy-start.2
  25.5 43.2 %collective-permute-start.11 = (bf16[128,1152]{1,0:T(8,128)(2,1)S(1)}, bf16[128,1152]{1,0:T(8,128)(2,1)S(1)}, u32[]{:S(2)}, u32[]{:S(2)}) collective-permute-start(bf16[128,1152]{1,0:T(8,128)(2,1)S(1)} %convolution_convert_fusion.3), channel_id=1, source_target_pairs={{0,1},{1,0},{2,3},{3,2},{4,5},{5,4},{6,7},{7,6},{8,9},{9,8},{10,11... | collective-permute-start | bytes 884744 | tf_op jit(solution)/shard_map/ppermute | solution.py:16
  29.8 43.4 %collective-permute-start.8 = (bf16[128,1152]{1,0:T(8,128)(2,1)S(1)}, bf16[128,1152]{1,0:T(8,128)(2,1)S(1)}, u32[]{:S(2)}, u32[]{:S(2)}) collective-permute-start(bf16[128,1152]{1,0:T(8,128)(2,1)S(1)} %convolution_convert_fusion.5), channel_id=1, source_target_pairs={{0,16},{16,0},{8,24},{24,8},{32,48},{48,32},{40,56},{56,40},{64,80... | collective-permute-start | bytes 884744 | tf_op jit(solution)/shard_map/ppermute | solution.py:16
  34.1 9.9 %collective-permute-start.5 = (bf16[128,1152]{1,0:T(8,128)(2,1)S(1)}, bf16[128,1152]{1,0:T(8,128)(2,1)S(1)}, u32[]{:S(2)}, u32[]{:S(2)}) collective-permute-start(bf16[128,1152]{1,0:T(8,128)(2,1)S(1)} %collective-permute-done.1), channel_id=1, source_target_pairs={{0,1},{1,0},{2,3},{3,2},{4,5},{5,4},{6,7},{7,6},{8,9},{9,8},{10,11... | collective-permute-start | bytes 884744 | tf_op jit(solution)/shard_map/ppermute | solution.py:16
  36.3 18.0 %collective-permute-start.2 = (bf16[128,1152]{1,0:T(8,128)(2,1)S(1)}, bf16[128,1152]{1,0:T(8,128)(2,1)S(1)}, u32[]{:S(2)}, u32[]{:S(2)}) collective-permute-start(bf16[128,1152]{1,0:T(8,128)(2,1)S(1)} %collective-permute-done), channel_id=1, source_target_pairs={{0,16},{16,0},{8,24},{24,8},{32,48},{48,32},{40,56},{56,40},{64,80... | collective-permute-start | bytes 884744 | tf_op jit(solution)/shard_map/ppermute | solution.py:16
  38.2 12.1 %collective-permute-start.4 = (bf16[128,1152]{1,0:T(8,128)(2,1)S(1)}, bf16[128,1152]{1,0:T(8,128)(2,1)S(1)}, u32[]{:S(2)}, u32[]{:S(2)}) collective-permute-start(bf16[128,1152]{1,0:T(8,128)(2,1)S(1)} %collective-permute-done), channel_id=1, source_target_pairs={{0,1},{1,0},{2,3},{3,2},{4,5},{5,4},{6,7},{7,6},{8,9},{9,8},{10,11... | collective-permute-start | bytes 884744 | tf_op jit(solution)/shard_map/ppermute | solution.py:16
  44.7 31.2 %collective-permute-start.14 = (bf16[128,1152]{1,0:T(8,128)(2,1)S(1)}, bf16[128,1152]{1,0:T(8,128)(2,1)S(1)}, u32[]{:S(2)}, u32[]{:S(2)}) collective-permute-start(bf16[128,1152]{1,0:T(8,128)(2,1)S(1)} %convolution_convert_fusion.1), channel_id=1, source_target_pairs={{0,16},{16,0},{8,24},{24,8},{32,48},{48,32},{40,56},{56,40},{64,80... | collective-permute-start | bytes 884744 | tf_op jit(solution)/shard_map/ppermute | solution.py:16
  51.0 28.0 %collective-permute-start.12 = (bf16[128,1152]{1,0:T(8,128)(2,1)S(1)}, bf16[128,1152]{1,0:T(8,128)(2,1)S(1)}, u32[]{:S(2)}, u32[]{:S(2)}) collective-permute-start(bf16[128,1152]{1,0:T(8,128)(2,1)S(1)} %convolution_convert_fusion.2), channel_id=1, source_target_pairs={{0,8},{8,0},{16,24},{24,16},{32,40},{40,32},{48,56},{56,48},{64,72... | collective-permute-start | bytes 884744 | tf_op jit(solution)/shard_map/ppermute | solution.py:16
  54.3 10.5 %collective-permute-start.6 = (bf16[128,1152]{1,0:T(8,128)(2,1)S(1)}, bf16[128,1152]{1,0:T(8,128)(2,1)S(1)}, u32[]{:S(2)}, u32[]{:S(2)}) collective-permute-start(bf16[128,1152]{1,0:T(8,128)(2,1)S(1)} %collective-permute-done.2), channel_id=1, source_target_pairs={{0,1},{1,0},{2,3},{3,2},{4,5},{5,4},{6,7},{7,6},{8,9},{9,8},{10,11... | collective-permute-start | bytes 884744 | tf_op jit(solution)/shard_map/ppermute | solution.py:16
  65.5 5.2 %collective-permute-start.16 = (bf16[128,1152]{1,0:T(8,128)(2,1)S(1)}, bf16[128,1152]{1,0:T(8,128)(2,1)S(1)}, u32[]{:S(2)}, u32[]{:S(2)}) collective-permute-start(bf16[128,1152]{1,0:T(8,128)(2,1)S(1)} %convolution_convert_fusion), channel_id=1, source_target_pairs={{0,8},{8,0},{16,24},{24,16},{32,40},{40,32},{48,56},{56,48},{64,72... | collective-permute-start | bytes 884744 | tf_op jit(solution)/shard_map/ppermute | solution.py:16
  68.8 12.5 %collective-permute-start.9 = (bf16[128,1152]{1,0:T(8,128)(2,1)S(1)}, bf16[128,1152]{1,0:T(8,128)(2,1)S(1)}, u32[]{:S(2)}, u32[]{:S(2)}) collective-permute-start(bf16[128,1152]{1,0:T(8,128)(2,1)S(1)} %convolution_convert_fusion.4), channel_id=1, source_target_pairs={{0,8},{8,0},{16,24},{24,16},{32,40},{40,32},{48,56},{56,48},{64,72... | collective-permute-start | bytes 884744 | tf_op jit(solution)/shard_map/ppermute | solution.py:16
  70.7 13.9 %collective-permute-start.17 = (bf16[128,1152]{1,0:T(8,128)(2,1)S(1)}, bf16[128,1152]{1,0:T(8,128)(2,1)S(1)}, u32[]{:S(2)}, u32[]{:S(2)}) collective-permute-start(bf16[128,1152]{1,0:T(8,128)(2,1)S(1)} %collective-permute-done.16), channel_id=1, source_target_pairs={{0,16},{16,0},{8,24},{24,8},{32,48},{48,32},{40,56},{56,40},{64,80... | collective-permute-start | bytes 884744 | tf_op jit(solution)/shard_map/ppermute | solution.py:16
  73.2 14.4 %collective-permute-start.7 = (bf16[128,1152]{1,0:T(8,128)(2,1)S(1)}, bf16[128,1152]{1,0:T(8,128)(2,1)S(1)}, u32[]{:S(2)}, u32[]{:S(2)}) collective-permute-start(bf16[128,1152]{1,0:T(8,128)(2,1)S(1)} %convolution_convert_fusion.6), channel_id=1, source_target_pairs={{0,8},{8,0},{16,24},{24,16},{32,40},{40,32},{48,56},{56,48},{64,72... | collective-permute-start | bytes 884744 | tf_op jit(solution)/shard_map/ppermute | solution.py:16
  75.9 11.7 %collective-permute-start.15 = (bf16[128,1152]{1,0:T(8,128)(2,1)S(1)}, bf16[128,1152]{1,0:T(8,128)(2,1)S(1)}, u32[]{:S(2)}, u32[]{:S(2)}) collective-permute-start(bf16[128,1152]{1,0:T(8,128)(2,1)S(1)} %collective-permute-done.14), channel_id=1, source_target_pairs={{0,1},{1,0},{2,3},{3,2},{4,5},{5,4},{6,7},{7,6},{8,9},{9,8},{10,11... | collective-permute-start | bytes 884744 | tf_op jit(solution)/shard_map/ppermute | solution.py:16
  79.0 13.7 %collective-permute-start.13 = (bf16[128,1152]{1,0:T(8,128)(2,1)S(1)}, bf16[128,1152]{1,0:T(8,128)(2,1)S(1)}, u32[]{:S(2)}, u32[]{:S(2)}) collective-permute-start(bf16[128,1152]{1,0:T(8,128)(2,1)S(1)} %collective-permute-done.12), channel_id=1, source_target_pairs={{0,1},{1,0},{2,3},{3,2},{4,5},{5,4},{6,7},{7,6},{8,9},{9,8},{10,11... | collective-permute-start | bytes 884744 | tf_op jit(solution)/shard_map/ppermute | solution.py:16
  81.2 11.5 %collective-permute-start.10 = (bf16[128,1152]{1,0:T(8,128)(2,1)S(1)}, bf16[128,1152]{1,0:T(8,128)(2,1)S(1)}, u32[]{:S(2)}, u32[]{:S(2)}) collective-permute-start(bf16[128,1152]{1,0:T(8,128)(2,1)S(1)} %collective-permute-done.9), channel_id=1, source_target_pairs={{0,16},{16,0},{8,24},{24,8},{32,48},{48,32},{40,56},{56,40},{64,80... | collective-permute-start | bytes 884744 | tf_op jit(solution)/shard_map/ppermute | solution.py:16
  84.6 14.4 %collective-permute-start.18 = (bf16[128,1152]{1,0:T(8,128)(2,1)S(1)}, bf16[128,1152]{1,0:T(8,128)(2,1)S(1)}, u32[]{:S(2)}, u32[]{:S(2)}) collective-permute-start(bf16[128,1152]{1,0:T(8,128)(2,1)S(1)} %collective-permute-done.17), channel_id=1, source_target_pairs={{0,1},{1,0},{2,3},{3,2},{4,5},{5,4},{6,7},{7,6},{8,9},{9,8},{10,11... | collective-permute-start | bytes 884744 | tf_op jit(solution)/shard_map/ppermute | solution.py:16
where the time goes:
time: 101 us
  starting transfers between devices  61.7 us (61%)
  waiting for transfers between devices  25 us (25%)
  matrix products  6.88 us (7%)
  other arithmetic  3.99 us (4%)
  between operations  2.41 us (2%)
    ppermute x19, starting transfers between devices, swapped(): return lax.ppermute(block, axis, route)  61.7 us
    ppermute x19, waiting for transfers between devices, swapped(): return lax.ppermute(block, axis, route)  25 us
    dot_general x8, matrix products, on_device(): jnp.dot(image_half_rows, block.T, preferred_element_type=jnp.float32)  2.54 us
    dot_general x8, matrix products, on_device(): lax.dot_general(coef, image_half_rows, (((0,), (0,)), ((), ())), preferre...  2.43 us
    broadcast_in_dim x2, other arithmetic, on_device(): return (picture_derivative[None], text_grad[None])  2.06 us
  transfers between devices with their start and end apart: 19, of which 5 were waited for; matrix products, arithmetic and copies ran while one was open for 8% of the time, Pallas kernels for 0%

commit v1 on v0

v1 whole, which is shorter than its diff:
```python
import jax
import jax.numpy as jnp
from jax import lax
from jax.sharding import PartitionSpec as P

AXES = ("dp", "group")


def routes(n_dp, n_group):
    core, first, second = [], [], []
    for d in range(n_dp):
        for g in range(n_group):
            here = d * n_group + g
            over_core = (d ^ 1) * n_group + g
            over_z = (d ^ 2) * n_group + g
            over_y = d * n_group + (g ^ 1)
            core.append((here, over_core))
            first.append((here, over_z if d & 1 else over_y))
            second.append((here, over_y if d & 1 else over_z))
    return core, first, second


def normalize(values):
    wide = values.astype(jnp.float32)
    inverse = lax.rsqrt(jnp.sum(wide * wide, axis=-1, keepdims=True) + 1e-06)
    return wide * inverse, inverse


def finish(vectors, inverse, grad):
    return (grad - vectors * jnp.sum(vectors * grad, axis=-1, keepdims=True)) * inverse


def matmul_nt(a, b):
    return lax.dot_general(a, b, (((1,), (1,)), ((), ())), preferred_element_type=jnp.float32)


def matmul_nn(a, b):
    return lax.dot_general(a, b, (((1,), (0,)), ((), ())), preferred_element_type=jnp.float32)


def matmul_tn(a, b):
    return lax.dot_general(a, b, (((0,), (0,)), ((), ())), preferred_element_type=jnp.float32)


def on_device(x, y, slot, sharpness, offset):
    core_route, first_route, second_route = routes(lax.axis_size("dp"), lax.axis_size("group"))
    on_first_core = (lax.axis_index("dp") & 1) == 0
    scale, shift = sharpness[0], offset[0]
    xn, inv_x = normalize(x[0])
    yn, inv_y = normalize(y[0])
    xb, yb = xn.astype(jnp.bfloat16), yn.astype(jnp.bfloat16)
    a_own = jnp.where(on_first_core, xb, yb)
    b_own = jnp.where(on_first_core, yb, xb)
    a_far = lax.ppermute(a_own, AXES, first_route)
    b_far = lax.ppermute(b_own, AXES, second_route)
    other = lax.ppermute(jnp.stack([a_own, b_own]), AXES, core_route)
    b_oth, a_oth = other[0], other[1]

    count = xb.shape[0]
    rows = lax.broadcasted_iota(jnp.int32, (count, count), 0)
    columns = lax.broadcasted_iota(jnp.int32, (count, count), 1)
    slots = slot[0, 0]
    positive = jnp.where(on_first_core, slots[:, None] == columns, slots[None, :] == rows)

    def coef(a, b, mask=None):
        logits = scale * matmul_nt(a, b) + shift
        if mask is None:
            return (scale * jax.nn.sigmoid(logits)).astype(jnp.bfloat16)
        sign = jnp.where(mask, 1.0, -1.0)
        return (-scale * sign * jax.nn.sigmoid(-sign * logits)).astype(jnp.bfloat16)

    c_own = coef(a_own, b_own, positive)
    c_own_oth = coef(a_own, b_oth)
    c_oth_own = coef(a_oth, b_own)
    ga_own = matmul_nn(c_own, b_own) + matmul_nn(c_own_oth, b_oth)
    gb_own = matmul_tn(c_own, a_own) + matmul_tn(c_oth_own, a_oth)

    b_far_oth = lax.ppermute(a_far, AXES, core_route)
    c_far_own = coef(a_far, b_own)
    ga_far = matmul_nn(c_far_own, b_own) + matmul_nn(coef(a_far, b_oth), b_oth)
    gb_own = gb_own + matmul_tn(c_far_own, a_far)
    ga_own = ga_own + matmul_nn(coef(a_own, b_far_oth), b_far_oth)
    ga_far = ga_far + matmul_nn(coef(a_far, b_far_oth), b_far_oth)

    a_far_oth = lax.ppermute(b_far, AXES, core_route)
    c_far_far = coef(a_far, b_far)
    ga_far = ga_far + matmul_nn(c_far_far, b_far)
    ga_back = lax.ppermute(ga_far.astype(jnp.bfloat16), AXES, first_route)
    c_own_far = coef(a_own, b_far)
    gb_far = (
        matmul_tn(c_far_far, a_far)
        + matmul_tn(c_own_far, a_own)
        + matmul_tn(coef(a_oth, b_far), a_oth)
        + matmul_tn(coef(a_far_oth, b_far), a_far_oth)
    )
    gb_back = lax.ppermute(gb_far.astype(jnp.bfloat16), AXES, second_route)
    ga_own = ga_own + matmul_nn(c_own_far, b_far)
    gb_own = gb_own + matmul_tn(coef(a_far_oth, b_own), a_far_oth)

    ga = ga_own + ga_back.astype(jnp.float32)
    gb = gb_own + gb_back.astype(jnp.float32)
    gx = jnp.where(on_first_core, ga, gb)
    gy = jnp.where(on_first_core, gb, ga)
    return finish(xn, inv_x, gx)[None], finish(yn, inv_y, gy)[None]


def solution(mesh):
    spec = P("group", "dp", None)
    return jax.shard_map(
        on_device,
        mesh=mesh,
        in_specs=(spec, spec, spec, P(), P()),
        out_specs=(spec, spec),
        check_vma=False,
    )
```

time: 101 us -> 66.8 us (0.66)
  starting transfers between devices: 61.7 us -> 31 us
  waiting for transfers between devices: 25 us -> 0.02 us
  matrix products: 6.88 us -> 28.4 us
    ppermute x19 -> x7, starting transfers between devices: 61.7 us -> 31 us  [the longest x1 13.9 us: on_device(): other = lax.ppermute(jnp.stack([a_own, b_own]), AXES, core_route)]
    ppermute x19 -> x7, waiting for transfers between devices: 25 us -> 0.02 us  [the longest x1 0.01 us: on_device(): b_far = lax.ppermute(b_own, AXES, second_route)]
    dot_general x24 -> x20, matrix products: 6.88 us -> 28.4 us  [the longest x8 14.9 us: matmul_tn(): lax.dot_general(a, b, (((0,), (0,)), ((), ())), preferred_element_type=jn...]
    broadcast_in_dim x2 -> x1, other arithmetic: 2.06 us -> 1.29 us  [on_device(): return (finish(xn, inv_x, gx)[None], finish(yn, inv_y, gy)[None])]
  transfers between devices with their start and end apart: 19 -> 7, of which waited for: 5 -> 0; matrix products, arithmetic and copies ran while one was open for 8% -> 42% of each run, Pallas kernels for 0% -> 0%
where the time goes in v1:
time: 66.8 us; the launch traced here: 66.1 us
  starting transfers between devices  31 us (46%)
  matrix products  28.4 us (43%)
  other arithmetic  3.9 us (6%)
  between operations  2.13 us (3%)
  local copies, waits for them, and re-layouts  0.67 us (1%)
    dot_general x8, matrix products, matmul_tn(): lax.dot_general(a, b, (((0,), (0,)), ((), ())), preferred_element_type=jn...  14.9 us
    ppermute x1, starting transfers between devices, on_device(): other = lax.ppermute(jnp.stack([a_own, b_own]), AXES, core_route)  13.9 us
    dot_general x8, matrix products, matmul_nn(): lax.dot_general(a, b, (((1,), (0,)), ((), ())), preferred_element_type=jn...  12.4 us
    ppermute x1, starting transfers between devices, on_device(): b_far = lax.ppermute(b_own, AXES, second_route)  4.03 us
    ppermute x1, starting transfers between devices, on_device(): a_far = lax.ppermute(a_own, AXES, first_route)  3.64 us
    ppermute x1, starting transfers between devices, on_device(): ga_back = lax.ppermute(ga_far.astype(jnp.bfloat16), AXES, first_route)  3.15 us
    ppermute x1, starting transfers between devices, on_device(): b_far_oth = lax.ppermute(a_far, AXES, core_route)  2.41 us
    ppermute x1, starting transfers between devices, on_device(): a_far_oth = lax.ppermute(b_far, AXES, core_route)  1.91 us
  transfers between devices with their start and end apart: 7, of which 0 were waited for; matrix products, arithmetic and copies ran while one was open for 42% of the time, Pallas kernels for 0%

profile of v1, /device:TPU:1, one launch (start us, length us, event | category | flops | bytes accessed | tf_op | source)
XLA Modules:
  0.0 66.1 jit_solution(14351939199313024537)
XLA Ops:
  0.7 1.2 %fusion.107 = f32[128]{0:T(128)S(1)} fusion(bf16[1,128,1152]{2,1,0:T(8,128)(2,1)} %param.5), kind=kLoop, calls=%fused_computation.132 | loop fusion | flops 442240 | bytes 295424 | tf_op jit(solution)/shard_map/reduce_sum | solution.py:25
  2.2 4.0 %collective-permute-start.3 = (bf16[128,1152]{1,0:T(8,128)(2,1)S(1)}, bf16[128,1152]{1,0:T(8,128)(2,1)S(1)}, u32[]{:S(2)}, u32[]{:S(2)}) collective-permute-start(bf16[128,1152]{1,0:T(8,128)(2,1)S(1)} %get-tuple-element.6), channel_id=1, source_target_pairs={{0,16},{1,17},{2,18},{3,19},{4,20},{5,21},{6,22},{7,23},{8,9},{9,8... | collective-permute-start | bytes 884744 | tf_op jit(solution)/shard_map/ppermute | solution.py:55
  7.3 13.9 %collective-permute-start = (bf16[2,128,1152]{2,1,0:T(8,128)(2,1)}, bf16[2,128,1152]{2,1,0:T(8,128)(2,1)S(1)}, u32[]{:S(2)}, u32[]{:S(2)}) collective-permute-start(bf16[2,128,1152]{2,1,0:T(8,128)(2,1)} %pad_maximum_fusion), channel_id=1, source_target_pairs={{0,8},{1,9},{2,10},{3,11},{4,12},{5,13},{6,14},{7,15},{8,0},{9,1},... | collective-permute-start | bytes 1769480 | tf_op jit(solution)/shard_map/ppermute | solution.py:56
  21.3 3.6 %collective-permute-start.1 = (bf16[128,1152]{1,0:T(8,128)(2,1)S(1)}, bf16[128,1152]{1,0:T(8,128)(2,1)S(1)}, u32[]{:S(2)}, u32[]{:S(2)}) collective-permute-start(bf16[128,1152]{1,0:T(8,128)(2,1)S(1)} %get-tuple-element.7), channel_id=1, source_target_pairs={{0,1},{1,0},{2,3},{3,2},{4,5},{5,4},{6,7},{7,6},{8,24},{9,25},{10,... | collective-permute-start | bytes 884744 | tf_op jit(solution)/shard_map/ppermute | solution.py:54
  27.2 1.1 %fusion.158 = f32[128,1152]{1,0:T(8,128)} fusion(bf16[128,128]{1,0:T(8,128)(2,1)S(1)} %fusion.80, bf16[128,1152]{1,0:T(8,128)(2,1)S(1)} %get-tuple-element.7), kind=kOutput, calls=%fused_computation.196 | convolution fusion | flops 37748736 | bytes 917504 | tf_op jit(solution)/shard_map/dot_general | solution.py:42
  28.3 1.0 %fusion.154 = f32[128,1152]{1,0:T(8,128)} fusion(bf16[128,128]{1,0:T(8,128)(2,1)S(1)} %fusion.80, bf16[128,1152]{1,0:T(8,128)(2,1)S(1)} %get-tuple-element.6), kind=kOutput, calls=%fused_computation.192 | convolution fusion | flops 37748736 | bytes 917504 | tf_op jit(solution)/shard_map/dot_general | solution.py:38
  29.6 1.1 %fusion.159 = f32[128,1152]{1,0:T(8,128)} fusion(bf16[128,128]{1,0:T(8,128)(2,1)S(1)} %fusion.83, bf16[128,1152]{1,0:T(8,128)(2,1)S(1)} %get-tuple-element.7), kind=kOutput, calls=%fused_computation.197 | convolution fusion | flops 37748736 | bytes 917504 | tf_op jit(solution)/shard_map/dot_general | solution.py:42
  30.9 1.1 %fusion.156 = f32[128,1152]{1,0:T(8,128)} fusion(bf16[128,128]{1,0:T(8,128)(2,1)S(1)} %fusion.84, bf16[128,1152]{1,0:T(8,128)(2,1)S(1)} %get-tuple-element.6), kind=kOutput, calls=%fused_computation.194 | convolution fusion | flops 37748736 | bytes 917504 | tf_op jit(solution)/shard_map/dot_general | solution.py:38
  32.0 1.9 %collective-permute-start.5 = (bf16[128,1152]{1,0:T(8,128)(2,1)S(1)}, bf16[128,1152]{1,0:T(8,128)(2,1)S(1)}, u32[]{:S(2)}, u32[]{:S(2)}) collective-permute-start(bf16[128,1152]{1,0:T(8,128)(2,1)S(1)} %collective-permute-done.3), channel_id=1, source_target_pairs={{0,8},{1,9},{2,10},{3,11},{4,12},{5,13},{6,14},{7,15},{8,0},{9,1},... | collective-permute-start | bytes 884744 | tf_op jit(solution)/shard_map/ppermute | solution.py:85
  33.9 2.4 %collective-permute-start.2 = (bf16[128,1152]{1,0:T(8,128)(2,1)S(1)}, bf16[128,1152]{1,0:T(8,128)(2,1)S(1)}, u32[]{:S(2)}, u32[]{:S(2)}) collective-permute-start(bf16[128,1152]{1,0:T(8,128)(2,1)S(1)} %collective-permute-done.1), channel_id=1, source_target_pairs={{0,8},{1,9},{2,10},{3,11},{4,12},{5,13},{6,14},{7,15},{8,0},{9,1},... | collective-permute-start | bytes 884744 | tf_op jit(solution)/shard_map/ppermute | solution.py:78
  36.6 1.0 %fusion.155 = f32[128,1152]{1,0:T(8,128)} fusion(bf16[128,128]{1,0:T(8,128)(2,1)S(1)} %fusion.83, bf16[128,1152]{1,0:T(8,128)(2,1)S(1)} %collective-permute-done.3), kind=kOutput, calls=%fused_computation.193 | convolution fusion | flops 37748736 | bytes 917504 | tf_op jit(solution)/shard_map/dot_general | solution.py:38
  38.7 1.4 %fusion.92 = f32[128,1152]{1,0:T(8,128)} fusion(bf16[128,1152]{1,0:T(8,128)(2,1)S(1)} %collective-permute-done.3, bf16[2,128,1152]{2,1,0:T(8,128)(2,1)S(1)} %collective-permute-done, f32[]{:T(128)} %bitcast.134, f32[]{:T(128)} %bitcast.121), kind=kOutput, calls=%fused_computation.113 | convolution fusion | flops 75612160 | bytes 1474568 | tf_op jit(solution)/shard_map/dot_general | solution.py:42
  40.2 2.4 %fusion = f32[128,1152]{1,0:T(8,128)} fusion(f32[128,1152]{1,0:T(8,128)} %fusion.92, f32[128,1152]{1,0:T(8,128)} %fusion.159, bf16[128,128]{1,0:T(8,128)(2,1)} %copy-done.2, bf16[128,1152]{1,0:T(8,128)(2,1)S(1)} %collective-permute-done.1), kind=kOutput, calls=%fused_computation.2 | convolution fusion | flops 38043648 | bytes 2097152 | tf_op jit(solution)/shard_map/dot_general | solution.py:42
  42.5 2.4 %fusion.6 = bf16[128,1152]{1,0:T(8,128)(2,1)} fusion(f32[128,1152]{1,0:T(8,128)} %fusion, bf16[128,1152]{1,0:T(8,128)(2,1)S(1)} %collective-permute-done.5, bf16[128,1152]{1,0:T(8,128)(2,1)S(1)} %collective-permute-done.3, f32[]{:T(128)} %bitcast.133, f32[]{:T(128)} %bitcast.125), kind=kOutput, calls=%fused_computation.15 | convolution fusion | flops 75907072 | bytes 1474568 | tf_op jit(solution)/shard_map/dot_general | solution.py:42
  44.9 1.9 %collective-permute-start.6 = (bf16[128,1152]{1,0:T(8,128)(2,1)}, bf16[128,1152]{1,0:T(8,128)(2,1)S(1)}, u32[]{:S(2)}, u32[]{:S(2)}) collective-permute-start(bf16[128,1152]{1,0:T(8,128)(2,1)} %fusion.6), channel_id=1, source_target_pairs={{0,16},{1,17},{2,18},{3,19},{4,20},{5,21},{6,22},{7,23},{8,9},{9,8... | collective-permute-start | bytes 884744 | tf_op jit(solution)/shard_map/ppermute | solution.py:96
  46.8 2.5 %convolution_add_fusion.6 = f32[128,1152]{1,0:T(8,128)} fusion(f32[128,1152]{1,0:T(8,128)} %fusion.156, bf16[128,1152]{1,0:T(8,128)(2,1)S(1)} %collective-permute-done.1, bf16[2,128,1152]{2,1,0:T(8,128)(2,1)S(1)} %collective-permute-done, f32[]{:T(128)} %bitcast.139, f32[]{:T(128)} %bitcast.122), kind=kOutput, calls=%fused_computation.9 | convolution fusion | flops 75759616 | bytes 2064392 | tf_op jit(solution)/shard_map/dot_general | solution.py:38
  49.3 2.5 %fusion.5 = bf16[128,1152]{1,0:T(8,128)(2,1)} fusion(f32[128,1152]{1,0:T(8,128)} %fusion.157, f32[128,1152]{1,0:T(8,128)} %convolution_add_fusion.6, bf16[128,1152]{1,0:T(8,128)(2,1)S(1)} %collective-permute-done.2, bf16[128,1152]{1,0:T(8,128)(2,1)S(1)} %collective-permute-done.1, f32[]{:T(128)} %bitcast.138, f32[]{:T(128)} %bitcast.131), kind=kOutput, calls=%fused_computation.14 | convolution fusion | flops 76054528 | bytes 2064392 | tf_op jit(solution)/shard_map/dot_general | solution.py:38
  51.8 3.1 %collective-permute-start.4 = (bf16[128,1152]{1,0:T(8,128)(2,1)}, bf16[128,1152]{1,0:T(8,128)(2,1)}, u32[]{:S(2)}, u32[]{:S(2)}) collective-permute-start(bf16[128,1152]{1,0:T(8,128)(2,1)} %fusion.5), channel_id=1, source_target_pairs={{0,1},{1,0},{2,3},{3,2},{4,5},{5,4},{6,7},{7,6},{8,24},{9,25},{10,... | collective-permute-start | bytes 884744 | tf_op jit(solution)/shard_map/ppermute | solution.py:88
  55.0 2.5 %convolution_add_fusion.4 = f32[128,1152]{1,0:T(8,128)} fusion(f32[128,1152]{1,0:T(8,128)} %fusion.158, bf16[1,128,1152]{2,1,0:T(8,128)(2,1)S(1)} %get-tuple-element.9, bf16[2,128,1152]{2,1,0:T(8,128)(2,1)S(1)} %collective-permute-done, f32[]{:T(128)} %bitcast.136, f32[]{:T(128)} %bitcast.123), kind=kOutput, calls=%fused_computation.6 | convolution fusion | flops 75759616 | bytes 2064392 | tf_op jit(solution)/shard_map/dot_general | solution.py:42
  57.5 2.2 %convolution_add_fusion.3 = f32[128,1152]{1,0:T(8,128)} fusion(f32[128,1152]{1,0:T(8,128)} %convolution_add_fusion.4, bf16[128,128]{1,0:T(8,128)(2,1)} %copy-done.3, bf16[128,1152]{1,0:T(8,128)(2,1)S(1)} %collective-permute-done.1), kind=kOutput, calls=%fused_computation.5 | convolution fusion | flops 37896192 | bytes 1507328 | tf_op jit(solution)/shard_map/dot_general | solution.py:42
  59.6 1.6 %convolution_add_fusion.8 = f32[128,1152]{1,0:T(8,128)S(1)} fusion(f32[128,1152]{1,0:T(8,128)} %fusion.154, bf16[1,128,1152]{2,1,0:T(8,128)(2,1)S(1)} %get-tuple-element.8, bf16[2,128,1152]{2,1,0:T(8,128)(2,1)S(1)} %collective-permute-done, f32[]{:T(128)} %bitcast.143, f32[]{:T(128)} %bitcast.130), kind=kOutput, calls=%fused_computation.13 | convolution fusion | flops 75759616 | bytes 2064392 | tf_op jit(solution)/shard_map/dot_general | solution.py:38
  61.2 1.7 %fusion.4 = f32[128,1152]{1,0:T(8,128)S(1)} fusion(f32[128,1152]{1,0:T(8,128)} %fusion.155, f32[128,1152]{1,0:T(8,128)S(1)} %convolution_add_fusion.8, bf16[128,1152]{1,0:T(8,128)(2,1)S(1)} %collective-permute-done.2, bf16[128,1152]{1,0:T(8,128)(2,1)S(1)} %get-tuple-element.7, bf16[128,1152]{1,0:T(8,128)(2,1)} %collective-permute-done.4, f32[]{:T(128)} %bitcast.142, ...), kind=kOutput, calls=%fused_computation.12 | convolution fusion | flops 76201984 | bytes 2654216 | tf_op jit(solution)/shard_map/dot_general | solution.py:38
  63.0 1.8 %fusion.109 = (f32[128]{0:T(128)S(1)}, f32[128]{0:T(128)S(1)}, f32[128,1152]{1,0:T(8,128)S(1)}) fusion(bf16[1,128,1152]{2,1,0:T(8,128)(2,1)S(1)} %copy-done, f32[128]{0:T(128)S(1)} %get-tuple-element.11, f32[128,1152]{1,0:T(8,128)S(1)} %fusion.4, pred[]{:T(512)S(6)} %eq.21, f32[128]{0:T(128)S(1)} %get-tuple-element.12, ...), kind=kOutput, calls=%fused_computation.134 | convolution fusion | flops 77528832 | bytes 3246089 | tf_op jit(solution)/shard_map/dot_general | solution.py:42
  64.8 1.3 %fusion.112 = (f32[1,128,1152]{2,1,0:T(8,128)}, f32[1,128,1152]{2,1,0:T(8,128)}) fusion(bf16[1,128,1152]{2,1,0:T(8,128)(2,1)S(1)} %copy-done, f32[128]{0:T(128)S(1)} %get-tuple-element.2, f32[128]{0:T(128)S(1)} %get-tuple-element.11, f32[128,1152]{1,0:T(8,128)S(1)} %get-tuple-element.10, f32[128,1152]{1,0:T(8,128)S(1)} %fusion.4, pred[]{:T(512)S(6)} %eq.21, ...), kind=kLoop, calls=%fused_computation.137 | loop fusion | flops 1769472 | bytes 2951169 | tf_op jit(solution)/shard_map/broadcast_in_dim | solution.py:104
  (27 shorter events, 4.2 us)
Async XLA Ops:
  0.6 1.2 %copy-start = (bf16[1,128,1152]{2,1,0:T(8,128)(2,1)S(1)}, bf16[1,128,1152]{2,1,0:T(8,128)(2,1)}, u32[]{:S(2)}) copy-start(bf16[1,128,1152]{2,1,0:T(8,128)(2,1)} %param.6) | copy-start | bytes 884740
  0.6 1.3 %copy-start.1 = (bf16[1,128,1152]{2,1,0:T(8,128)(2,1)S(1)}, bf16[1,128,1152]{2,1,0:T(8,128)(2,1)}, u32[]{:S(2)}) copy-start(bf16[1,128,1152]{2,1,0:T(8,128)(2,1)} %param.5) | copy-start | bytes 884740
  2.2 27.1 %collective-permute-start.3 = (bf16[128,1152]{1,0:T(8,128)(2,1)S(1)}, bf16[128,1152]{1,0:T(8,128)(2,1)S(1)}, u32[]{:S(2)}, u32[]{:S(2)}) collective-permute-start(bf16[128,1152]{1,0:T(8,128)(2,1)S(1)} %get-tuple-element.6), channel_id=1, source_target_pairs={{0,16},{1,17},{2,18},{3,19},{4,20},{5,21},{6,22},{7,23},{8,9},{9,8... | collective-permute-start | bytes 884744 | tf_op jit(solution)/shard_map/ppermute | solution.py:55
  7.3 31.4 %collective-permute-start = (bf16[2,128,1152]{2,1,0:T(8,128)(2,1)}, bf16[2,128,1152]{2,1,0:T(8,128)(2,1)S(1)}, u32[]{:S(2)}, u32[]{:S(2)}) collective-permute-start(bf16[2,128,1152]{2,1,0:T(8,128)(2,1)} %pad_maximum_fusion), channel_id=1, source_target_pairs={{0,8},{1,9},{2,10},{3,11},{4,12},{5,13},{6,14},{7,15},{8,0},{9,1},... | collective-permute-start | bytes 1769480 | tf_op jit(solution)/shard_map/ppermute | solution.py:56
  21.3 9.4 %collective-permute-start.1 = (bf16[128,1152]{1,0:T(8,128)(2,1)S(1)}, bf16[128,1152]{1,0:T(8,128)(2,1)S(1)}, u32[]{:S(2)}, u32[]{:S(2)}) collective-permute-start(bf16[128,1152]{1,0:T(8,128)(2,1)S(1)} %get-tuple-element.7), channel_id=1, source_target_pairs={{0,1},{1,0},{2,3},{3,2},{4,5},{5,4},{6,7},{7,6},{8,24},{9,25},{10,... | collective-permute-start | bytes 884744 | tf_op jit(solution)/shard_map/ppermute | solution.py:54
  26.2 0.7 copy-start.4
  30.9 1.1 %copy-start.3 = (bf16[128,128]{1,0:T(8,128)(2,1)}, bf16[128,128]{1,0:T(8,128)(2,1)S(1)}, u32[]{:S(2)}) copy-start(bf16[128,128]{1,0:T(8,128)(2,1)S(1)} %fusion.84) | copy-start | bytes 98308
  32.0 10.5 %collective-permute-start.5 = (bf16[128,1152]{1,0:T(8,128)(2,1)S(1)}, bf16[128,1152]{1,0:T(8,128)(2,1)S(1)}, u32[]{:S(2)}, u32[]{:S(2)}) collective-permute-start(bf16[128,1152]{1,0:T(8,128)(2,1)S(1)} %collective-permute-done.3), channel_id=1, source_target_pairs={{0,8},{1,9},{2,10},{3,11},{4,12},{5,13},{6,14},{7,15},{8,0},{9,1},... | collective-permute-start | bytes 884744 | tf_op jit(solution)/shard_map/ppermute | solution.py:85
  33.9 15.4 %collective-permute-start.2 = (bf16[128,1152]{1,0:T(8,128)(2,1)S(1)}, bf16[128,1152]{1,0:T(8,128)(2,1)S(1)}, u32[]{:S(2)}, u32[]{:S(2)}) collective-permute-start(bf16[128,1152]{1,0:T(8,128)(2,1)S(1)} %collective-permute-done.1), channel_id=1, source_target_pairs={{0,8},{1,9},{2,10},{3,11},{4,12},{5,13},{6,14},{7,15},{8,0},{9,1},... | collective-permute-start | bytes 884744 | tf_op jit(solution)/shard_map/ppermute | solution.py:78
  36.6 1.1 %copy-start.2 = (bf16[128,128]{1,0:T(8,128)(2,1)}, bf16[128,128]{1,0:T(8,128)(2,1)S(1)}, u32[]{:S(2)}) copy-start(bf16[128,128]{1,0:T(8,128)(2,1)S(1)} %fusion.87) | copy-start | bytes 98308
  44.9 18.0 %collective-permute-start.6 = (bf16[128,1152]{1,0:T(8,128)(2,1)}, bf16[128,1152]{1,0:T(8,128)(2,1)S(1)}, u32[]{:S(2)}, u32[]{:S(2)}) collective-permute-start(bf16[128,1152]{1,0:T(8,128)(2,1)} %fusion.6), channel_id=1, source_target_pairs={{0,16},{1,17},{2,18},{3,19},{4,20},{5,21},{6,22},{7,23},{8,9},{9,8... | collective-permute-start | bytes 884744 | tf_op jit(solution)/shard_map/ppermute | solution.py:96
  51.8 9.4 %collective-permute-start.4 = (bf16[128,1152]{1,0:T(8,128)(2,1)}, bf16[128,1152]{1,0:T(8,128)(2,1)}, u32[]{:S(2)}, u32[]{:S(2)}) collective-permute-start(bf16[128,1152]{1,0:T(8,128)(2,1)} %fusion.5), channel_id=1, source_target_pairs={{0,1},{1,0},{2,3},{3,2},{4,5},{5,4},{6,7},{7,6},{8,24},{9,25},{10,... | collective-permute-start | bytes 884744 | tf_op jit(solution)/shard_map/ppermute | solution.py:88

commit v2 on v1

v2 whole, which is shorter than its diff:
```python
import functools

import jax
import jax.numpy as jnp
from jax import lax
from jax.experimental import pallas as pl
from jax.experimental.pallas import tpu as pltpu
from jax.sharding import PartitionSpec as P

AXES = ("dp", "group")
HERE = pl.BlockSpec(memory_space=pltpu.VMEM)
AFAR = pl.BlockSpec(memory_space=pltpu.HBM)
SHORT = pl.CostEstimate(flops=1, bytes_accessed=1, transcendentals=0)
LONG = pl.CostEstimate(flops=30_000_000_000, bytes_accessed=1, transcendentals=0)
PARAMS = pltpu.CompilerParams(vmem_limit_bytes=32 * 1024 * 1024)
CHUNK = 32


def routes(n_dp, n_group):
    core, first, second = [], [], []
    for d in range(n_dp):
        for g in range(n_group):
            here = d * n_group + g
            over_core = (d ^ 1) * n_group + g
            over_z = (d ^ 2) * n_group + g
            over_y = d * n_group + (g ^ 1)
            core.append((here, over_core))
            first.append((here, over_z if d & 1 else over_y))
            second.append((here, over_y if d & 1 else over_z))
    return core, first, second


def core_of():
    return lax.axis_index("dp") & 1


def load_chunks(x_ref, y_ref, swap, raw, sems):
    copies = []
    for k in range(raw.shape[0] // CHUNK):
        at = pl.ds(k * CHUNK, CHUNK)
        from_x = pltpu.make_async_copy(x_ref.at[0, at], raw.at[at], sems.at[k])
        from_y = pltpu.make_async_copy(y_ref.at[0, at], raw.at[at], sems.at[k])
        pl.when(swap == 0)(from_x.start)
        pl.when(swap != 0)(from_y.start)
        copies.append((at, from_x))
    return copies


def unit(raw):
    wide = raw.astype(jnp.float32)
    inverse = lax.rsqrt(jnp.sum(wide * wide, axis=-1, keepdims=True) + 1e-06)
    return wide * inverse, inverse


def first_kernel(x_ref, y_ref, a_ref, raw, sems):
    for at, copy in load_chunks(x_ref, y_ref, core_of(), raw, sems):
        copy.wait()
        a_ref[at] = unit(raw[at])[0].astype(a_ref.dtype)


def second_kernel(x_ref, y_ref, a_ref, b_ref, raw, sems):
    for at, copy in load_chunks(x_ref, y_ref, 1 - core_of(), raw, sems):
        copy.wait()
        b_ref[at] = unit(raw[at])[0].astype(b_ref.dtype)


def copy_kernel(in_ref, out_ref):
    out_ref[...] = in_ref[...]


def pack_kernel(scale_ref, shift_ref, a_ref, a1_ref, b_ref, pack_ref, pair_ref):
    for k, ref in enumerate((scale_ref, shift_ref)):
        pair_ref[k] = jnp.full(pair_ref.shape[1:], ref[0])
    for k, ref in enumerate((a_ref, a1_ref, b_ref)):
        pack_ref[k] = ref[...]


def joined(refs):
    return jnp.concatenate([ref[...] for ref in refs], axis=0)


def weigh(q, keys, scale, shift, positive=None):
    logits = scale * lax.dot_general(
        q, keys, (((1,), (1,)), ((), ())), preferred_element_type=jnp.float32
    ) + shift
    if positive is None:
        return (scale * jax.nn.sigmoid(logits)).astype(jnp.bfloat16)
    wide = positive.shape[1]
    sign = jnp.where(positive, 1.0, -1.0)
    near = -scale * sign * jax.nn.sigmoid(-sign * logits[:, :wide])
    rest = scale * jax.nn.sigmoid(logits[:, wide:])
    return jnp.concatenate([near, rest], axis=1).astype(jnp.bfloat16)


def scalars_of(pair_ref):
    return pair_ref[0, 0:1, 0:1], pair_ref[1, 0:1, 0:1]


def collect(coef, key_refs, out_ref, tile=384):
    for start in range(0, out_ref.shape[-1], tile):
        at = pl.ds(start, tile)
        keys = jnp.concatenate([ref[:, at] for ref in key_refs], axis=0)
        total = jnp.dot(coef, keys, preferred_element_type=jnp.float32)
        out_ref[:, at] = total.astype(out_ref.dtype)


def partial_kernel(pair_ref, pack_ref, other_ref, b2_ref, a2_ref, out_ref):
    if a2_ref is None:
        q, keys = pack_ref.at[1], (pack_ref.at[2], other_ref.at[0], other_ref.at[1], b2_ref)
    else:
        q, keys = b2_ref, (pack_ref.at[0], pack_ref.at[1], other_ref.at[2], a2_ref)
    coef = weigh(q[...], joined(keys), *scalars_of(pair_ref))
    collect(coef, keys, out_ref)


def partial_a(pair_ref, pack_ref, other_ref, b2_ref, out_ref):
    partial_kernel(pair_ref, pack_ref, other_ref, b2_ref, None, out_ref)


def own_kernel(
    pair_ref, slot_ref, x_ref, y_ref, pack_ref, other_ref, b2_ref, a2_ref,
    ga_ref, gb_ref, an_ref, bn_ref, ia_ref, ib_ref, raw_a, raw_b, slots, sems_a, sems_b, sem,
):
    core = core_of()
    copies_a = load_chunks(x_ref, y_ref, core, raw_a, sems_a)
    copies_b = load_chunks(x_ref, y_ref, 1 - core, raw_b, sems_b)
    load = pltpu.make_async_copy(slot_ref.at[0], slots, sem)
    load.start()
    scale, shift = scalars_of(pair_ref)
    count = raw_a.shape[0]
    rows = lax.broadcasted_iota(jnp.int32, (count, count), 0)
    load.wait()
    across = jnp.broadcast_to(slots[...], (count, count))
    by_text = (across == rows).astype(jnp.float32)
    by_image = by_text.T
    first = core == 0
    mask_a = jnp.where(first, by_image, by_text) > 0.5
    mask_b = jnp.where(first, by_text, by_image) > 0.5
    a_ref, a1_ref, b_ref = (pack_ref.at[k] for k in range(3))
    b_oth, b1_ref, a_oth = (other_ref.at[k] for k in range(3))
    b_keys = (b_ref, b_oth, b1_ref, b2_ref)
    a_keys = (a_ref, a_oth, a1_ref, a2_ref)
    collect(weigh(a_ref[...], joined(b_keys), scale, shift, mask_a), b_keys, ga_ref)
    collect(weigh(b_ref[...], joined(a_keys), scale, shift, mask_b), a_keys, gb_ref)
    for copies, raw, n_ref, i_ref in (
        (copies_a, raw_a, an_ref, ia_ref), (copies_b, raw_b, bn_ref, ib_ref),
    ):
        for at, copy in copies:
            copy.wait()
            vectors, inverse = unit(raw[at])
            n_ref[at] = vectors
            i_ref[at] = jnp.broadcast_to(inverse, (CHUNK, i_ref.shape[1]))


def project(g_ref, back, n_ref, i_ref, done, here, there, sems, first):
    copies = []
    for k in range(done.shape[0] // CHUNK):
        at = pl.ds(k * CHUNK, CHUNK)
        grad = g_ref[at] + back[at].astype(jnp.float32)
        vectors = n_ref[at]
        along = jnp.sum(vectors * grad, axis=-1, keepdims=True)
        done[at] = (grad - vectors * along) * i_ref[at, 0:1]
        to_here = pltpu.make_async_copy(done.at[at], here.at[0, at], sems.at[k])
        to_there = pltpu.make_async_copy(done.at[at], there.at[0, at], sems.at[k])
        pl.when(first)(to_here.start)
        pl.when(jnp.logical_not(first))(to_there.start)
        copies.append(to_here)
    for copy in copies:
        copy.wait()


def project_a(g_ref, back, n_ref, i_ref, x_out, y_out, done, sems):
    project(g_ref, back, n_ref, i_ref, done, x_out, y_out, sems, core_of() == 0)


def project_b(g_ref, back, n_ref, i_ref, x_in, y_in, x_out, y_out, done, sems):
    project(g_ref, back, n_ref, i_ref, done, y_out, x_out, sems, core_of() == 0)


def on_device(x, y, slot, scale, shift):
    core_route, first_route, second_route = routes(lax.axis_size("dp"), lax.axis_size("group"))
    _, count, width = x.shape
    chunks = count // CHUNK
    half = jax.ShapeDtypeStruct((count, width), jnp.bfloat16)
    wide = jax.ShapeDtypeStruct((count, width), jnp.float32)
    lanes = jax.ShapeDtypeStruct((count, 128), jnp.float32)
    loads = [pltpu.VMEM((count, width), jnp.bfloat16), pltpu.SemaphoreType.DMA((chunks,))]

    pack = jax.ShapeDtypeStruct((3, count, width), jnp.bfloat16)
    call = functools.partial(pl.pallas_call, compiler_params=PARAMS, cost_estimate=SHORT)
    x, y, slot = (
        pltpu.with_memory_space_constraint(v, pltpu.HBM) for v in (x, y, slot)
    )

    a = call(
        first_kernel, out_shape=half, in_specs=[AFAR] * 2, out_specs=HERE,
        scratch_shapes=loads, name="normalize_a",
    )(x, y)
    a1 = lax.ppermute(a, AXES, first_route)
    b = call(
        second_kernel, out_shape=half, in_specs=[AFAR, AFAR, HERE], out_specs=HERE,
        scratch_shapes=loads, name="normalize_b",
    )(x, y, a)
    b2 = lax.ppermute(b, AXES, second_route)
    mine, pair = call(
        pack_kernel, out_shape=(pack, jax.ShapeDtypeStruct((2, 8, 128), jnp.float32)),
        in_specs=[pl.BlockSpec(memory_space=pltpu.SMEM)] * 2 + [HERE] * 3,
        out_specs=(HERE, HERE), name="pack",
    )(scale, shift, a, a1, b)
    other = lax.ppermute(mine, AXES, core_route)
    held = call(
        copy_kernel, out_shape=half, in_specs=[HERE], out_specs=HERE, name="copy_b2",
        cost_estimate=LONG,
    )(b2)
    a2 = lax.ppermute(held, AXES, core_route)

    part_a = call(
        partial_a, out_shape=half, in_specs=[HERE] * 4, out_specs=HERE, name="partial_a"
    )(pair, mine, other, b2)
    back_a = lax.ppermute(part_a, AXES, first_route)
    part_b = call(
        partial_kernel, out_shape=half, in_specs=[HERE] * 5, out_specs=HERE, name="partial_b"
    )(pair, mine, other, b2, a2)
    back_b = lax.ppermute(part_b, AXES, second_route)
    ga, gb, an, bn, ia, ib = call(
        own_kernel, out_shape=(wide, wide, wide, wide, lanes, lanes),
        in_specs=[HERE] + [AFAR] * 3 + [HERE] * 4, out_specs=(HERE,) * 6,
        scratch_shapes=[
            loads[0], loads[0], pltpu.VMEM((1, count), jnp.int32),
            loads[1], loads[1], pltpu.SemaphoreType.DMA,
        ],
        name="own",
    )(pair, slot, x, y, mine, other, b2, a2)
    out = jax.ShapeDtypeStruct(x.shape, jnp.float32)
    stores = [pltpu.VMEM((count, width), jnp.float32), pltpu.SemaphoreType.DMA((chunks,))]
    outs = call(
        project_a, out_shape=(out, out), in_specs=[HERE] * 4, out_specs=(AFAR, AFAR),
        scratch_shapes=stores, name="project_a",
    )(ga, back_a, an, ia)
    return call(
        project_b, out_shape=(out, out), in_specs=[HERE] * 4 + [AFAR] * 2,
        out_specs=(AFAR, AFAR), scratch_shapes=stores,
        input_output_aliases={4: 0, 5: 1}, name="project_b",
    )(gb, back_b, bn, ib, *outs)


def solution(mesh):
    spec = P("group", "dp", None)
    return jax.shard_map(
        on_device,
        mesh=mesh,
        in_specs=(spec, spec, spec, P(), P()),
        out_specs=(spec, spec),
        check_vma=False,
    )
```

time: 66.8 us -> 43.8 us (0.66)
  matrix products: 28.4 us -> 0 us
  Pallas kernels: 0 us -> 10.2 us
  other arithmetic: 3.9 us -> 0 us
  local copies, waits for them, and re-layouts: 0.67 us -> 0 us
    dot_general x20 -> x0, matrix products: 28.4 us -> none  [the longest x8 14.9 us: matmul_tn(): lax.dot_general(a, b, (((0,), (0,)), ((), ())), preferred_element_type=jn...]
    pallas_call x0 -> x9, Pallas kernels: none -> 10.2 us  [the longest x1 3.49 us: on_device(): call(own_kernel, out_shape=(wide, wide, wide, wide, lanes, lanes), in_spe...]
    reduce_sum x2 -> x0, other arithmetic: 1.31 us -> none  [normalize(): inverse = lax.rsqrt(jnp.sum(wide * wide, axis=-1, keepdims=True) + 1e-06)]
    broadcast_in_dim x1 -> x0, other arithmetic: 1.29 us -> none  [on_device(): return (finish(xn, inv_x, gx)[None], finish(yn, inv_y, gy)[None])]
    another operation x1 -> x0, other arithmetic: 0.9 us -> none  [on_device(): other = lax.ppermute(jnp.stack([a_own, b_own]), AXES, core_route)]
    ppermute x7 -> x6, starting transfers between devices: 31 us -> 30.8 us  [the longest x1 14.4 us: on_device(): other = lax.ppermute(mine, AXES, core_route)]
  transfers between devices with their start and end apart: 7 -> 6, of which waited for: 0 -> 1; matrix products, arithmetic and copies ran while one was open for 42% -> 0% of each run, Pallas kernels for 0% -> 18%
where the time goes in v2:
time: 43.8 us; the launch traced here: 43.3 us
  starting transfers between devices  30.8 us (70%)
  Pallas kernels  10.2 us (23%)
  between operations  2.07 us (5%)
    ppermute x1, starting transfers between devices, on_device(): other = lax.ppermute(mine, AXES, core_route)  14.4 us
    ppermute x1, starting transfers between devices, on_device(): a1 = lax.ppermute(a, AXES, first_route)  4.38 us
    ppermute x1, starting transfers between devices, on_device(): back_b = lax.ppermute(part_b, AXES, second_route)  3.64 us
    pallas_call x1, Pallas kernels, on_device(): call(own_kernel, out_shape=(wide, wide, wide, wide, lanes, lanes), in_spe...  3.49 us
    ppermute x1, starting transfers between devices, on_device(): b2 = lax.ppermute(b, AXES, second_route)  3.2 us
    ppermute x1, starting transfers between devices, on_device(): a2 = lax.ppermute(held, AXES, core_route)  3.2 us
    ppermute x1, starting transfers between devices, on_device(): back_a = lax.ppermute(part_a, AXES, first_route)  1.92 us
    pallas_call x1, Pallas kernels, on_device(): call(first_kernel, out_shape=half, in_specs=[AFAR] * 2, out_specs=HERE, s...  1.36 us
  transfers between devices with their start and end apart: 6, of which 1 were waited for; matrix products, arithmetic and copies ran while one was open for 0% of the time, Pallas kernels for 18%

profile of v2, /device:TPU:1, one launch (start us, length us, event | category | flops | bytes accessed | tf_op | source)
XLA Modules:
  0.0 43.3 jit_solution(622711118235039841)
XLA Ops:
  0.6 1.4 %normalize_a.1.a_ref = bf16[128,1152]{1,0:T(8,128)(2,1)S(1)} custom-call(bf16[1,128,1152]{2,1,0:T(8,128)(2,1)} %x_ref.5, bf16[1,128,1152]{2,1,0:T(8,128)(2,1)} %y_ref.5), custom_call_target="tpu_custom_call" | custom-call | flops 1 | bytes 1 | tf_op jit(solution)/shard_map/normalize_a/pallas_call | solution.py:195
  2.0 4.4 %collective-permute-start = (bf16[128,1152]{1,0:T(8,128)(2,1)S(1)}, bf16[128,1152]{1,0:T(8,128)(2,1)S(1)}, u32[]{:S(2)}, u32[]{:S(2)}) collective-permute-start(bf16[128,1152]{1,0:T(8,128)(2,1)S(1)} %normalize_a.1.a_ref), channel_id=1, source_target_pairs={{0,1},{1,0},{2,3},{3,2},{4,5},{5,4},{6,7},{7,6},{8,24},{9,25},{10,... | collective-permute-start | bytes 884744 | tf_op jit(solution)/shard_map/ppermute | solution.py:199
  6.4 1.4 %normalize_b.1.b_ref = bf16[128,1152]{1,0:T(8,128)(2,1)S(1)} custom-call(bf16[1,128,1152]{2,1,0:T(8,128)(2,1)} %x_ref.5, bf16[1,128,1152]{2,1,0:T(8,128)(2,1)} %y_ref.5, bf16[128,1152]{1,0:T(8,128)(2,1)S(1)} %normalize_a.1.a_ref), custom_call_target="tpu_custom_call" | custom-call | flops 1 | bytes 1 | tf_op jit(solution)/shard_map/normalize_b/pallas_call | solution.py:200
  7.7 3.2 %collective-permute-start.2 = (bf16[128,1152]{1,0:T(8,128)(2,1)S(1)}, bf16[128,1152]{1,0:T(8,128)(2,1)S(1)}, u32[]{:S(2)}, u32[]{:S(2)}) collective-permute-start(bf16[128,1152]{1,0:T(8,128)(2,1)S(1)} %normalize_b.1.b_ref), channel_id=1, source_target_pairs={{0,16},{1,17},{2,18},{3,19},{4,20},{5,21},{6,22},{7,23},{8,9},{9,8... | collective-permute-start | bytes 884744 | tf_op jit(solution)/shard_map/ppermute | solution.py:204
  12.3 0.0 collective-permute-done.a1_ref
  12.3 0.1 pack.1
  12.3 14.4 %collective-permute-start.1 = (bf16[3,128,1152]{2,1,0:T(8,128)(2,1)S(1)}, bf16[3,128,1152]{2,1,0:T(8,128)(2,1)S(1)}, u32[]{:S(2)}, u32[]{:S(2)}) collective-permute-start(bf16[3,128,1152]{2,1,0:T(8,128)(2,1)S(1)} %get-tuple-element.13.pack_ref), channel_id=1, source_target_pairs={{0,8},{1,9},{2,10},{3,11},{4,12},{5,13},{6,14},{7,15},{8,0},{9,1},... | collective-permute-start | bytes 2654216 | tf_op jit(solution)/shard_map/ppermute | solution.py:210
  26.8 0.0 collective-permute-done.2.in_ref.b2_ref
  26.8 3.2 %collective-permute-start.3 = (bf16[128,1152]{1,0:T(8,128)(2,1)S(1)}, bf16[128,1152]{1,0:T(8,128)(2,1)S(1)}, u32[]{:S(2)}, u32[]{:S(2)}) collective-permute-start(bf16[128,1152]{1,0:T(8,128)(2,1)S(1)} %copy_b2.1), channel_id=1, source_target_pairs={{0,8},{1,9},{2,10},{3,11},{4,12},{5,13},{6,14},{7,15},{8,0},{9,1},... | collective-permute-start | bytes 884744 | tf_op jit(solution)/shard_map/ppermute | solution.py:215
  30.0 0.0 collective-permute-done.1.other_ref
  30.0 0.9 %partial_a.1 = bf16[128,1152]{1,0:T(8,128)(2,1)S(1)} custom-call(f32[2,8,128]{2,1,0:T(8,128)S(1)} %get-tuple-element.12.pair_ref, bf16[3,128,1152]{2,1,0:T(8,128)(2,1)S(1)} %get-tuple-element.13.pack_ref, bf16[3,128,1152]{2,1,0:T(8,128)(2,1)S(1)} %collective-permute-done.1.other_ref, bf16[128,1152]{1,0:T(8,128)(2,1)S(1)} %collective-permute-done.2.in_ref.b2_ref), custom_call_target="tpu_custom_call" | custom-call | flops 1 | bytes 1 | tf_op jit(solution)/shard_map/partial_a/pallas_call | solution.py:217
  30.9 1.9 %collective-permute-start.5 = (bf16[128,1152]{1,0:T(8,128)(2,1)S(1)}, bf16[128,1152]{1,0:T(8,128)(2,1)S(1)}, u32[]{:S(2)}, u32[]{:S(2)}) collective-permute-start(bf16[128,1152]{1,0:T(8,128)(2,1)S(1)} %partial_a.1), channel_id=1, source_target_pairs={{0,1},{1,0},{2,3},{3,2},{4,5},{5,4},{6,7},{7,6},{8,24},{9,25},{10,... | collective-permute-start | bytes 884744 | tf_op jit(solution)/shard_map/ppermute | solution.py:220
  32.8 0.0 collective-permute-done.3.a2_ref
  32.8 0.9 %partial_b.1 = bf16[128,1152]{1,0:T(8,128)(2,1)S(1)} custom-call(f32[2,8,128]{2,1,0:T(8,128)S(1)} %get-tuple-element.12.pair_ref, bf16[3,128,1152]{2,1,0:T(8,128)(2,1)S(1)} %get-tuple-element.13.pack_ref, bf16[3,128,1152]{2,1,0:T(8,128)(2,1)S(1)} %collective-permute-done.1.other_ref, bf16[128,1152]{1,0:T(8,128)(2,1)S(1)} %collective-permute-done.2.in_ref.b2_ref, ...), custom_call_target="tpu_custom_call" | custom-call | flops 1 | bytes 1 | tf_op jit(solution)/shard_map/partial_b/pallas_call | solution.py:221
  33.7 3.6 %collective-permute-start.4 = (bf16[128,1152]{1,0:T(8,128)(2,1)S(1)}, bf16[128,1152]{1,0:T(8,128)(2,1)S(1)}, u32[]{:S(2)}, u32[]{:S(2)}) collective-permute-start(bf16[128,1152]{1,0:T(8,128)(2,1)S(1)} %partial_b.1), channel_id=1, source_target_pairs={{0,16},{1,17},{2,18},{3,19},{4,20},{5,21},{6,22},{7,23},{8,9},{9,8... | collective-permute-start | bytes 884744 | tf_op jit(solution)/shard_map/ppermute | solution.py:224
  37.4 3.5 %own.1 = (f32[128,1152]{1,0:T(8,128)S(1)}, f32[128,1152]{1,0:T(8,128)S(1)}, f32[128,1152]{1,0:T(8,128)S(1)}, f32[128,1152]{1,0:T(8,128)S(1)}, f32[128,128]{1,0:T(8,128)S(1)}, /*index=5*/f32[128,128]{1,0:T(8,128)S(1)}) custom-call(f32[2,8,128]{2,1,0:T(8,128)S(1)} %get-tuple-element.12.pair_ref, s32[1,1,128]{2,1,0:T(1,128)} %slot_ref.1, ...), custom_call_target="tpu_custom_call" | custom-call | flops 1 | bytes 1 | tf_op jit(solution)/shard_map/own/pallas_call | solution.py:225
  40.9 0.0 collective-permute-done.5.back
  40.9 1.1 %project_a.1 = (f32[1,128,1152]{2,1,0:T(8,128)}, f32[1,128,1152]{2,1,0:T(8,128)}) custom-call(f32[128,1152]{1,0:T(8,128)S(1)} %get-tuple-element.17.g_ref, bf16[128,1152]{1,0:T(8,128)(2,1)S(1)} %collective-permute-done.5.back, f32[128,1152]{1,0:T(8,128)S(1)} %get-tuple-element.18.n_ref, f32[128,128]{1,0:T(8,128)S(1)} %get-tuple-element.19.i_ref), custom_call_target="tpu_custom_call" | custom-call | flops 1 | bytes 1 | tf_op jit(solution)/shard_map/project_a/pallas_call | solution.py:236
  41.9 0.3 collective-permute-done.4.back
  42.3 1.0 %project_b.1 = (f32[1,128,1152]{2,1,0:T(8,128)}, f32[1,128,1152]{2,1,0:T(8,128)}) custom-call(f32[128,1152]{1,0:T(8,128)S(1)} %get-tuple-element.14.g_ref, bf16[128,1152]{1,0:T(8,128)(2,1)S(1)} %collective-permute-done.4.back, f32[128,1152]{1,0:T(8,128)S(1)} %get-tuple-element.15.n_ref, ...), custom_call_target="tpu_custom_call", output_to_operand_aliasing={{0}: (4, {}), {1}: (5, {})} | custom-call | flops 1 | bytes 1 | tf_op jit(solution)/shard_map/project_b/pallas_call | solution.py:240
  (1 shorter events, 0.0 us)
Async XLA Ops:
  2.0 10.3 %collective-permute-start = (bf16[128,1152]{1,0:T(8,128)(2,1)S(1)}, bf16[128,1152]{1,0:T(8,128)(2,1)S(1)}, u32[]{:S(2)}, u32[]{:S(2)}) collective-permute-start(bf16[128,1152]{1,0:T(8,128)(2,1)S(1)} %normalize_a.1.a_ref), channel_id=1, source_target_pairs={{0,1},{1,0},{2,3},{3,2},{4,5},{5,4},{6,7},{7,6},{8,24},{9,25},{10,... | collective-permute-start | bytes 884744 | tf_op jit(solution)/shard_map/ppermute | solution.py:199
  7.7 19.0 %collective-permute-start.2 = (bf16[128,1152]{1,0:T(8,128)(2,1)S(1)}, bf16[128,1152]{1,0:T(8,128)(2,1)S(1)}, u32[]{:S(2)}, u32[]{:S(2)}) collective-permute-start(bf16[128,1152]{1,0:T(8,128)(2,1)S(1)} %normalize_b.1.b_ref), channel_id=1, source_target_pairs={{0,16},{1,17},{2,18},{3,19},{4,20},{5,21},{6,22},{7,23},{8,9},{9,8... | collective-permute-start | bytes 884744 | tf_op jit(solution)/shard_map/ppermute | solution.py:204
  12.3 17.7 %collective-permute-start.1 = (bf16[3,128,1152]{2,1,0:T(8,128)(2,1)S(1)}, bf16[3,128,1152]{2,1,0:T(8,128)(2,1)S(1)}, u32[]{:S(2)}, u32[]{:S(2)}) collective-permute-start(bf16[3,128,1152]{2,1,0:T(8,128)(2,1)S(1)} %get-tuple-element.13.pack_ref), channel_id=1, source_target_pairs={{0,8},{1,9},{2,10},{3,11},{4,12},{5,13},{6,14},{7,15},{8,0},{9,1},... | collective-permute-start | bytes 2654216 | tf_op jit(solution)/shard_map/ppermute | solution.py:210
  26.8 6.0 %collective-permute-start.3 = (bf16[128,1152]{1,0:T(8,128)(2,1)S(1)}, bf16[128,1152]{1,0:T(8,128)(2,1)S(1)}, u32[]{:S(2)}, u32[]{:S(2)}) collective-permute-start(bf16[128,1152]{1,0:T(8,128)(2,1)S(1)} %copy_b2.1), channel_id=1, source_target_pairs={{0,8},{1,9},{2,10},{3,11},{4,12},{5,13},{6,14},{7,15},{8,0},{9,1},... | collective-permute-start | bytes 884744 | tf_op jit(solution)/shard_map/ppermute | solution.py:215
  30.9 10.0 %collective-permute-start.5 = (bf16[128,1152]{1,0:T(8,128)(2,1)S(1)}, bf16[128,1152]{1,0:T(8,128)(2,1)S(1)}, u32[]{:S(2)}, u32[]{:S(2)}) collective-permute-start(bf16[128,1152]{1,0:T(8,128)(2,1)S(1)} %partial_a.1), channel_id=1, source_target_pairs={{0,1},{1,0},{2,3},{3,2},{4,5},{5,4},{6,7},{7,6},{8,24},{9,25},{10,... | collective-permute-start | bytes 884744 | tf_op jit(solution)/shard_map/ppermute | solution.py:220
  33.7 8.6 %collective-permute-start.4 = (bf16[128,1152]{1,0:T(8,128)(2,1)S(1)}, bf16[128,1152]{1,0:T(8,128)(2,1)S(1)}, u32[]{:S(2)}, u32[]{:S(2)}) collective-permute-start(bf16[128,1152]{1,0:T(8,128)(2,1)S(1)} %partial_b.1), channel_id=1, source_target_pairs={{0,16},{1,17},{2,18},{3,19},{4,20},{5,21},{6,22},{7,23},{8,9},{9,8... | collective-permute-start | bytes 884744 | tf_op jit(solution)/shard_map/ppermute | solution.py:224

commit v3 on v2

v3 whole, which is shorter than its diff:
```python
import functools

import jax
import jax.numpy as jnp
from jax import lax
from jax.experimental import pallas as pl
from jax.experimental.pallas import tpu as pltpu
from jax.sharding import PartitionSpec as P

AXES = ("dp", "group")
HERE = pl.BlockSpec(memory_space=pltpu.VMEM)
AFAR = pl.BlockSpec(memory_space=pltpu.HBM)
SHORT = pl.CostEstimate(flops=1, bytes_accessed=1, transcendentals=0)
LONG = pl.CostEstimate(flops=8_000_000_000, bytes_accessed=1, transcendentals=0)
PARAMS = pltpu.CompilerParams(vmem_limit_bytes=32 * 1024 * 1024)
CHUNK = 128


def routes(n_dp, n_group):
    core, first, second, crossed = [], [], [], []
    for d in range(n_dp):
        for g in range(n_group):
            here = d * n_group + g
            over_core = (d ^ 1) * n_group + g
            over_z = (d ^ 2) * n_group + g
            over_y = d * n_group + (g ^ 1)
            core.append((here, over_core))
            first.append((here, over_z if d & 1 else over_y))
            second.append((here, over_y if d & 1 else over_z))
            cross_y, cross_z = (d ^ 1) * n_group + (g ^ 1), (d ^ 3) * n_group + g
            crossed.append((here, cross_y if d & 1 else cross_z))
    return core, first, second, crossed


def core_of():
    return lax.axis_index("dp") & 1


def load_chunks(x_ref, y_ref, swap, raw, sems):
    copies = []
    for k in range(raw.shape[0] // CHUNK):
        at = pl.ds(k * CHUNK, CHUNK)
        from_x = pltpu.make_async_copy(x_ref.at[0, at], raw.at[at], sems.at[k])
        from_y = pltpu.make_async_copy(y_ref.at[0, at], raw.at[at], sems.at[k])
        pl.when(swap == 0)(from_x.start)
        pl.when(swap != 0)(from_y.start)
        copies.append((at, from_x))
    return copies


def unit(raw):
    wide = raw.astype(jnp.float32)
    inverse = lax.rsqrt(jnp.sum(wide * wide, axis=-1, keepdims=True) + 1e-06)
    return wide * inverse, inverse


def first_kernel(
    x_ref, y_ref, a_ref, raw_a, raw_b, sems_a, sems_b
):
    core = core_of()
    copies_a = load_chunks(x_ref, y_ref, core, raw_a, sems_a)
    copies_b = load_chunks(x_ref, y_ref, 1 - core, raw_b, sems_b)
    for at, copy in copies_a:
        copy.wait()
        a_ref[at] = unit(raw_a[at])[0].astype(a_ref.dtype)
    for at, copy in copies_b:
        copy.wait()


def second_kernel(raw_ref, b_ref):
    for start in range(0, b_ref.shape[0], CHUNK):
        at = pl.ds(start, CHUNK)
        b_ref[at] = unit(raw_ref[at])[0].astype(b_ref.dtype)


def keep_kernel(a2_in, b2_in, a2_out, b2_out):
    b2_out[...] = b2_in[...]
    a2_out[...] = a2_in[...]


def pack_kernel(a_ref, a1_ref, b_ref, pack_ref):
    for k, ref in enumerate((a_ref, a1_ref, b_ref)):
        pack_ref[k] = ref[...]


def joined(refs):
    return jnp.concatenate([ref[...] for ref in refs], axis=0)


def weigh(q, keys, scale, shift, positive=None):
    logits = scale * lax.dot_general(
        q, keys, (((1,), (1,)), ((), ())), preferred_element_type=jnp.float32
    ) + shift
    if positive is None:
        return (scale * jax.nn.sigmoid(logits)).astype(jnp.bfloat16)
    wide = positive.shape[1]
    sign = jnp.where(positive, 1.0, -1.0)
    near = -scale * sign * jax.nn.sigmoid(-sign * logits[:, :wide])
    rest = scale * jax.nn.sigmoid(logits[:, wide:])
    return jnp.concatenate([near, rest], axis=1).astype(jnp.bfloat16)


def scalars_of(pair_ref):
    return pair_ref[0, 0:1, 0:1], pair_ref[1, 0:1, 0:1]


def collect(coef, key_refs, out_ref, tile=1152):
    for start in range(0, out_ref.shape[-1], tile):
        at = pl.ds(start, tile)
        keys = jnp.concatenate([ref[:, at] for ref in key_refs], axis=0)
        total = jnp.dot(coef, keys, preferred_element_type=jnp.float32)
        out_ref[:, at] = total.astype(out_ref.dtype)


def contribute(pair_ref, q_ref, keys, out_ref):
    coef = weigh(q_ref[...], joined(keys), *scalars_of(pair_ref))
    collect(coef, keys, out_ref)


def partial_a(pair_ref, pack_ref, other_ref, b2_ref, out_ref):
    keys = (pack_ref.at[2], other_ref.at[0], other_ref.at[1], b2_ref)
    contribute(pair_ref, pack_ref.at[1], keys, out_ref)


def partial_b(pair_ref, pack_ref, other_ref, b2_ref, a2_ref, out_ref):
    keys = (pack_ref.at[0], pack_ref.at[1], other_ref.at[2], a2_ref)
    contribute(pair_ref, b2_ref, keys, out_ref)


def norm_kernel(raw_a, raw_b, an_ref, bn_ref, ia_ref, ib_ref):
    for raw, n_ref, i_ref in ((raw_a, an_ref, ia_ref), (raw_b, bn_ref, ib_ref)):
        vectors, inverse = unit(raw[...])
        n_ref[...] = vectors
        i_ref[...] = jnp.broadcast_to(inverse, i_ref.shape)


def own_kernel(
    pair_ref, slot_ref, pack_ref, other_ref, b2_ref, a2_ref, ga_ref, gb_ref, slots, sem
):
    load = pltpu.make_async_copy(slot_ref.at[0], slots, sem)
    load.start()
    scale, shift = scalars_of(pair_ref)
    count = b2_ref.shape[0]
    rows = lax.broadcasted_iota(jnp.int32, (count, count), 0)
    load.wait()
    across = jnp.broadcast_to(slots[...], (count, count))
    by_text = (across == rows).astype(jnp.float32)
    by_image = by_text.T
    first = core_of() == 0
    mask_a = jnp.where(first, by_image, by_text) > 0.5
    mask_b = jnp.where(first, by_text, by_image) > 0.5
    a_ref, a1_ref, b_ref = (pack_ref.at[k] for k in range(3))
    b_oth, b1_ref, a_oth = (other_ref.at[k] for k in range(3))
    b_keys = (b_ref, b_oth, b1_ref, b2_ref)
    a_keys = (a_ref, a_oth, a1_ref, a2_ref)
    collect(weigh(a_ref[...], joined(b_keys), scale, shift, mask_a), b_keys, ga_ref)
    collect(weigh(b_ref[...], joined(a_keys), scale, shift, mask_b), a_keys, gb_ref)


def project(g_ref, back, n_ref, i_ref, done, here, there, sems, first):
    copies = []
    for k in range(done.shape[0] // CHUNK):
        at = pl.ds(k * CHUNK, CHUNK)
        grad = g_ref[at] + back[at].astype(jnp.float32)
        vectors = n_ref[at]
        along = jnp.sum(vectors * grad, axis=-1, keepdims=True)
        done[at] = (grad - vectors * along) * i_ref[at, 0:1]
        to_here = pltpu.make_async_copy(done.at[at], here.at[0, at], sems.at[k])
        to_there = pltpu.make_async_copy(done.at[at], there.at[0, at], sems.at[k])
        pl.when(first)(to_here.start)
        pl.when(jnp.logical_not(first))(to_there.start)
        copies.append(to_here)
    for copy in copies:
        copy.wait()


def project_a(g_ref, back, n_ref, i_ref, x_out, y_out, done, sems):
    project(g_ref, back, n_ref, i_ref, done, x_out, y_out, sems, core_of() == 0)


def project_b(g_ref, back, n_ref, i_ref, x_in, y_in, x_out, y_out, done, sems):
    project(g_ref, back, n_ref, i_ref, done, y_out, x_out, sems, core_of() == 0)


def on_device(x, y, slot, scale, shift):
    core_route, first_route, second_route, crossed_route = routes(
        lax.axis_size("dp"), lax.axis_size("group")
    )
    _, count, width = x.shape
    chunks = count // CHUNK
    half = jax.ShapeDtypeStruct((count, width), jnp.bfloat16)
    wide = jax.ShapeDtypeStruct((count, width), jnp.float32)
    lanes = jax.ShapeDtypeStruct((count, 128), jnp.float32)
    loads = pltpu.SemaphoreType.DMA((chunks,))

    pack = jax.ShapeDtypeStruct((3, count, width), jnp.bfloat16)
    call = functools.partial(pl.pallas_call, compiler_params=PARAMS, cost_estimate=SHORT)
    x, y, slot = (pltpu.with_memory_space_constraint(v, pltpu.HBM) for v in (x, y, slot))
    pair = jnp.stack([jnp.full((8, 128), scale[0]), jnp.full((8, 128), shift[0])])

    a, raw_a, raw_b = call(
        first_kernel, out_shape=(half,) * 3, in_specs=[AFAR] * 2, out_specs=(HERE,) * 3,
        scratch_shapes=[loads] * 2, name="normalize_a",
    )(x, y)
    a1 = lax.ppermute(a, AXES, first_route)
    b = call(
        second_kernel, out_shape=half, in_specs=[HERE], out_specs=HERE, name="normalize_b"
    )(raw_b)
    b2 = lax.ppermute(b, AXES, second_route)
    a2 = lax.ppermute(b, AXES, crossed_route)
    mine = call(
        pack_kernel, out_shape=pack, in_specs=[HERE] * 3, out_specs=HERE, name="pack"
    )(a, a1, b)
    other = lax.ppermute(mine, AXES, core_route)
    a2, b2 = call(
        keep_kernel, out_shape=(half, half), in_specs=[HERE] * 2, out_specs=(HERE, HERE),
        name="keep", cost_estimate=LONG,
    )(a2, b2)
    part_a = call(
        partial_a, out_shape=half, in_specs=[HERE] * 4, out_specs=HERE, name="partial_a"
    )(pair, mine, other, b2)
    back_a = lax.ppermute(part_a, AXES, first_route)
    part_b = call(
        partial_b, out_shape=half, in_specs=[HERE] * 5, out_specs=HERE, name="partial_b"
    )(pair, mine, other, b2, a2)
    back_b = lax.ppermute(part_b, AXES, second_route)
    an, bn, ia, ib = call(
        norm_kernel, out_shape=(wide, wide, lanes, lanes), in_specs=[HERE] * 2,
        out_specs=(HERE,) * 4, name="norms",
    )(raw_a, raw_b)
    ga, gb = call(
        own_kernel, out_shape=(wide, wide), in_specs=[HERE, AFAR] + [HERE] * 4,
        out_specs=(HERE,) * 2,
        scratch_shapes=[pltpu.VMEM((1, count), jnp.int32), pltpu.SemaphoreType.DMA],
        name="own",
    )(pair, slot, mine, other, b2, a2)
    out = jax.ShapeDtypeStruct(x.shape, jnp.float32)
    stores = [pltpu.VMEM((count, width), jnp.float32), pltpu.SemaphoreType.DMA((chunks,))]
    outs = call(
        project_a, out_shape=(out, out), in_specs=[HERE] * 4, out_specs=(AFAR, AFAR),
        scratch_shapes=stores, name="project_a",
    )(ga, back_a, an, ia)
    return call(
        project_b, out_shape=(out, out), in_specs=[HERE] * 4 + [AFAR] * 2,
        out_specs=(AFAR, AFAR), scratch_shapes=stores,
        input_output_aliases={4: 0, 5: 1}, name="project_b",
    )(gb, back_b, bn, ib, *outs)


def solution(mesh):
    spec = P("group", "dp", None)
    return jax.shard_map(
        on_device,
        mesh=mesh,
        in_specs=(spec, spec, spec, P(), P()),
        out_specs=(spec, spec),
        check_vma=False,
    )
```

time: 43.8 us -> 42.6 us (0.973)
  Pallas kernels: 10.2 us -> 7.67 us
  waiting for transfers between devices: 0.35 us -> 2.51 us
  starting transfers between devices: 30.8 us -> 30 us
    ppermute x1, starting transfers between devices: 14.4 us -> 2.97 us  [on_device(): other = lax.ppermute(mine, AXES, core_route)]
    ppermute x1, starting transfers between devices: 3.2 us -> 13.9 us  [on_device(): a2 = lax.ppermute(b, AXES, crossed_route)]
    pallas_call x6 -> x7, Pallas kernels: 7.18 us -> 4.69 us  [the longest x1 2.17 us: on_device(): call(own_kernel, out_shape=(wide, wide), in_specs=[HERE, AFAR] + [HERE] *...]
    ppermute x1, waiting for transfers between devices: 0.01 us -> 1.25 us  [on_device(): a2 = lax.ppermute(b, AXES, crossed_route)]
    ppermute x1, waiting for transfers between devices: 0.33 us -> 1.25 us  [on_device(): back_b = lax.ppermute(part_b, AXES, second_route)]
    ppermute x1, starting transfers between devices: 1.92 us -> 2.37 us  [on_device(): back_a = lax.ppermute(part_a, AXES, first_route)]
  transfers between devices with their start and end apart: 6 -> 6, of which waited for: 1 -> 2; matrix products, arithmetic and copies ran while one was open for 0% -> 0% of each run, Pallas kernels for 18% -> 11%
where the time goes in v3:
time: 42.6 us; the launch traced here: 42.3 us
  starting transfers between devices  30 us (70%)
  Pallas kernels  7.67 us (18%)
  waiting for transfers between devices  2.51 us (6%)
  between operations  2.07 us (5%)
    ppermute x1, starting transfers between devices, on_device(): a2 = lax.ppermute(b, AXES, crossed_route)  13.9 us
    ppermute x1, starting transfers between devices, on_device(): a1 = lax.ppermute(a, AXES, first_route)  4.38 us
    ppermute x1, starting transfers between devices, on_device(): back_b = lax.ppermute(part_b, AXES, second_route)  3.21 us
    ppermute x1, starting transfers between devices, on_device(): b2 = lax.ppermute(b, AXES, second_route)  3.2 us
    ppermute x1, starting transfers between devices, on_device(): other = lax.ppermute(mine, AXES, core_route)  2.97 us
    ppermute x1, starting transfers between devices, on_device(): back_a = lax.ppermute(part_a, AXES, first_route)  2.37 us
    pallas_call x1, Pallas kernels, on_device(): call(own_kernel, out_shape=(wide, wide), in_specs=[HERE, AFAR] + [HERE] *...  2.17 us
    ppermute x1, waiting for transfers between devices, on_device(): a2 = lax.ppermute(b, AXES, crossed_route)  1.25 us
  transfers between devices with their start and end apart: 6, of which 2 were waited for; matrix products, arithmetic and copies ran while one was open for 0% of the time, Pallas kernels for 11%

profile of v3, /device:TPU:1, one launch (start us, length us, event | category | flops | bytes accessed | tf_op | source)
XLA Modules:
  0.0 42.3 jit_solution(955682935067576356)
XLA Ops:
  0.6 1.2 %normalize_a.1 = (bf16[128,1152]{1,0:T(8,128)(2,1)S(1)}, bf16[128,1152]{1,0:T(8,128)(2,1)S(1)}, bf16[128,1152]{1,0:T(8,128)(2,1)S(1)}) custom-call(bf16[1,128,1152]{2,1,0:T(8,128)(2,1)} %x_ref.1, bf16[1,128,1152]{2,1,0:T(8,128)(2,1)} %y_ref.1), custom_call_target="tpu_custom_call" | custom-call | flops 1 | bytes 1 | tf_op jit(solution)/shard_map/normalize_a/pallas_call | solution.py:201
  1.9 4.4 %collective-permute-start = (bf16[128,1152]{1,0:T(8,128)(2,1)S(1)}, bf16[128,1152]{1,0:T(8,128)(2,1)S(1)}, u32[]{:S(2)}, u32[]{:S(2)}) collective-permute-start(bf16[128,1152]{1,0:T(8,128)(2,1)S(1)} %get-tuple-element.15.a_ref), channel_id=1, source_target_pairs={{0,1},{1,0},{2,3},{3,2},{4,5},{5,4},{6,7},{7,6},{8,24},{9,25},{10,... | collective-permute-start | bytes 884744 | tf_op jit(solution)/shard_map/ppermute | solution.py:205
  6.2 0.1 normalize_b.1.b_ref
  6.4 3.2 %collective-permute-start.3 = (bf16[128,1152]{1,0:T(8,128)(2,1)S(1)}, bf16[128,1152]{1,0:T(8,128)(2,1)S(1)}, u32[]{:S(2)}, u32[]{:S(2)}) collective-permute-start(bf16[128,1152]{1,0:T(8,128)(2,1)S(1)} %normalize_b.1.b_ref), channel_id=1, source_target_pairs={{0,16},{1,17},{2,18},{3,19},{4,20},{5,21},{6,22},{7,23},{8,9},{9,8... | collective-permute-start | bytes 884744 | tf_op jit(solution)/shard_map/ppermute | solution.py:209
  9.6 13.9 %collective-permute-start.2 = (bf16[128,1152]{1,0:T(8,128)(2,1)S(1)}, bf16[128,1152]{1,0:T(8,128)(2,1)S(1)}, u32[]{:S(2)}, u32[]{:S(2)}) collective-permute-start(bf16[128,1152]{1,0:T(8,128)(2,1)S(1)} %normalize_b.1.b_ref), channel_id=1, source_target_pairs={{0,24},{1,25},{2,26},{3,27},{4,28},{5,29},{6,30},{7,31},{8,1},{9,0... | collective-permute-start | bytes 884744 | tf_op jit(solution)/shard_map/ppermute | solution.py:210
  23.5 0.0 collective-permute-done.a1_ref
  23.5 0.1 pack.1.pack_ref
  23.6 3.0 %collective-permute-start.1 = (bf16[3,128,1152]{2,1,0:T(8,128)(2,1)S(1)}, bf16[3,128,1152]{2,1,0:T(8,128)(2,1)S(1)}, u32[]{:S(2)}, u32[]{:S(2)}) collective-permute-start(bf16[3,128,1152]{2,1,0:T(8,128)(2,1)S(1)} %pack.1.pack_ref), channel_id=1, source_target_pairs={{0,8},{1,9},{2,10},{3,11},{4,12},{5,13},{6,14},{7,15},{8,0},{9,1},... | collective-permute-start | bytes 2654216 | tf_op jit(solution)/shard_map/ppermute | solution.py:214
  27.8 0.0 collective-permute-done.3.b2_in
  27.8 1.3 %collective-permute-done.2.a2_in = bf16[128,1152]{1,0:T(8,128)(2,1)S(1)} collective-permute-done((bf16[128,1152]{1,0:T(8,128)(2,1)S(1)}, bf16[128,1152]{1,0:T(8,128)(2,1)S(1)}, u32[]{:S(2)}, u32[]{:S(2)}) %collective-permute-start.2) | collective-permute-done | bytes 294944 | tf_op jit(solution)/shard_map/ppermute | solution.py:210
  29.1 0.0 collective-permute-done.1.other_ref
  29.2 0.1 stack.6.pair_ref
  29.2 0.8 %partial_a.1 = bf16[128,1152]{1,0:T(8,128)(2,1)S(1)} custom-call(f32[2,8,128]{2,1,0:T(8,128)S(1)} %stack.6.pair_ref, bf16[3,128,1152]{2,1,0:T(8,128)(2,1)S(1)} %pack.1.pack_ref, bf16[3,128,1152]{2,1,0:T(8,128)(2,1)S(1)} %collective-permute-done.1.other_ref, bf16[128,1152]{1,0:T(8,128)(2,1)S(1)} %get-tuple-element.17.b2_ref), custom_call_target="tpu_custom_call" | custom-call | flops 1 | bytes 1 | tf_op jit(solution)/shard_map/partial_a/pallas_call | solution.py:219
  30.1 2.4 %collective-permute-start.5 = (bf16[128,1152]{1,0:T(8,128)(2,1)S(1)}, bf16[128,1152]{1,0:T(8,128)(2,1)S(1)}, u32[]{:S(2)}, u32[]{:S(2)}) collective-permute-start(bf16[128,1152]{1,0:T(8,128)(2,1)S(1)} %partial_a.1), channel_id=1, source_target_pairs={{0,1},{1,0},{2,3},{3,2},{4,5},{5,4},{6,7},{7,6},{8,24},{9,25},{10,... | collective-permute-start | bytes 884744 | tf_op jit(solution)/shard_map/ppermute | solution.py:222
  32.4 0.8 %partial_b.1 = bf16[128,1152]{1,0:T(8,128)(2,1)S(1)} custom-call(f32[2,8,128]{2,1,0:T(8,128)S(1)} %stack.6.pair_ref, bf16[3,128,1152]{2,1,0:T(8,128)(2,1)S(1)} %pack.1.pack_ref, bf16[3,128,1152]{2,1,0:T(8,128)(2,1)S(1)} %collective-permute-done.1.other_ref, bf16[128,1152]{1,0:T(8,128)(2,1)S(1)} %get-tuple-element.17.b2_ref, ...), custom_call_target="tpu_custom_call" | custom-call | flops 1 | bytes 1 | tf_op jit(solution)/shard_map/partial_b/pallas_call | solution.py:223
  33.3 3.2 %collective-permute-start.4 = (bf16[128,1152]{1,0:T(8,128)(2,1)S(1)}, bf16[128,1152]{1,0:T(8,128)(2,1)S(1)}, u32[]{:S(2)}, u32[]{:S(2)}) collective-permute-start(bf16[128,1152]{1,0:T(8,128)(2,1)S(1)} %partial_b.1), channel_id=1, source_target_pairs={{0,16},{1,17},{2,18},{3,19},{4,20},{5,21},{6,22},{7,23},{8,9},{9,8... | collective-permute-start | bytes 884744 | tf_op jit(solution)/shard_map/ppermute | solution.py:226
  36.5 0.2 norms.1
  36.7 2.2 %own.1 = (f32[128,1152]{1,0:T(8,128)S(1)}, f32[128,1152]{1,0:T(8,128)S(1)}) custom-call(f32[2,8,128]{2,1,0:T(8,128)S(1)} %stack.6.pair_ref, s32[1,1,128]{2,1,0:T(1,128)} %slot_ref.1, bf16[3,128,1152]{2,1,0:T(8,128)(2,1)S(1)} %pack.1.pack_ref, bf16[3,128,1152]{2,1,0:T(8,128)(2,1)S(1)} %collective-permute-done.1.other_ref, ...), custom_call_target="tpu_custom_call" | custom-call | flops 1 | bytes 1 | tf_op jit(solution)/shard_map/own/pallas_call | solution.py:231
  38.9 0.0 collective-permute-done.5.back
  38.9 1.1 %project_a.1 = (f32[1,128,1152]{2,1,0:T(8,128)}, f32[1,128,1152]{2,1,0:T(8,128)}) custom-call(f32[128,1152]{1,0:T(8,128)S(1)} %get-tuple-element.23.g_ref, bf16[128,1152]{1,0:T(8,128)(2,1)S(1)} %collective-permute-done.5.back, f32[128,1152]{1,0:T(8,128)S(1)} %get-tuple-element.24.n_ref, f32[128,128]{1,0:T(8,128)S(1)} %get-tuple-element.25.i_ref), custom_call_target="tpu_custom_call" | custom-call | flops 1 | bytes 1 | tf_op jit(solution)/shard_map/project_a/pallas_call | solution.py:239
  40.0 1.2 %collective-permute-done.4.back = bf16[128,1152]{1,0:T(8,128)(2,1)S(1)} collective-permute-done((bf16[128,1152]{1,0:T(8,128)(2,1)S(1)}, bf16[128,1152]{1,0:T(8,128)(2,1)S(1)}, u32[]{:S(2)}, u32[]{:S(2)}) %collective-permute-start.4) | collective-permute-done | bytes 294944 | tf_op jit(solution)/shard_map/ppermute | solution.py:226
  41.2 1.1 %project_b.1 = (f32[1,128,1152]{2,1,0:T(8,128)}, f32[1,128,1152]{2,1,0:T(8,128)}) custom-call(f32[128,1152]{1,0:T(8,128)S(1)} %get-tuple-element.19.g_ref, bf16[128,1152]{1,0:T(8,128)(2,1)S(1)} %collective-permute-done.4.back, f32[128,1152]{1,0:T(8,128)S(1)} %get-tuple-element.21.n_ref, ...), custom_call_target="tpu_custom_call", output_to_operand_aliasing={{0}: (4, {}), {1}: (5, {})} | custom-call | flops 1 | bytes 1 | tf_op jit(solution)/shard_map/project_b/pallas_call | solution.py:243
  (2 shorter events, 0.0 us)
Async XLA Ops:
  1.9 21.6 %collective-permute-start = (bf16[128,1152]{1,0:T(8,128)(2,1)S(1)}, bf16[128,1152]{1,0:T(8,128)(2,1)S(1)}, u32[]{:S(2)}, u32[]{:S(2)}) collective-permute-start(bf16[128,1152]{1,0:T(8,128)(2,1)S(1)} %get-tuple-element.15.a_ref), channel_id=1, source_target_pairs={{0,1},{1,0},{2,3},{3,2},{4,5},{5,4},{6,7},{7,6},{8,24},{9,25},{10,... | collective-permute-start | bytes 884744 | tf_op jit(solution)/shard_map/ppermute | solution.py:205
  6.4 21.4 %collective-permute-start.3 = (bf16[128,1152]{1,0:T(8,128)(2,1)S(1)}, bf16[128,1152]{1,0:T(8,128)(2,1)S(1)}, u32[]{:S(2)}, u32[]{:S(2)}) collective-permute-start(bf16[128,1152]{1,0:T(8,128)(2,1)S(1)} %normalize_b.1.b_ref), channel_id=1, source_target_pairs={{0,16},{1,17},{2,18},{3,19},{4,20},{5,21},{6,22},{7,23},{8,9},{9,8... | collective-permute-start | bytes 884744 | tf_op jit(solution)/shard_map/ppermute | solution.py:209
  9.6 19.5 %collective-permute-start.2 = (bf16[128,1152]{1,0:T(8,128)(2,1)S(1)}, bf16[128,1152]{1,0:T(8,128)(2,1)S(1)}, u32[]{:S(2)}, u32[]{:S(2)}) collective-permute-start(bf16[128,1152]{1,0:T(8,128)(2,1)S(1)} %normalize_b.1.b_ref), channel_id=1, source_target_pairs={{0,24},{1,25},{2,26},{3,27},{4,28},{5,29},{6,30},{7,31},{8,1},{9,0... | collective-permute-start | bytes 884744 | tf_op jit(solution)/shard_map/ppermute | solution.py:210
  23.6 5.6 %collective-permute-start.1 = (bf16[3,128,1152]{2,1,0:T(8,128)(2,1)S(1)}, bf16[3,128,1152]{2,1,0:T(8,128)(2,1)S(1)}, u32[]{:S(2)}, u32[]{:S(2)}) collective-permute-start(bf16[3,128,1152]{2,1,0:T(8,128)(2,1)S(1)} %pack.1.pack_ref), channel_id=1, source_target_pairs={{0,8},{1,9},{2,10},{3,11},{4,12},{5,13},{6,14},{7,15},{8,0},{9,1},... | collective-permute-start | bytes 2654216 | tf_op jit(solution)/shard_map/ppermute | solution.py:214
  30.1 8.8 %collective-permute-start.5 = (bf16[128,1152]{1,0:T(8,128)(2,1)S(1)}, bf16[128,1152]{1,0:T(8,128)(2,1)S(1)}, u32[]{:S(2)}, u32[]{:S(2)}) collective-permute-start(bf16[128,1152]{1,0:T(8,128)(2,1)S(1)} %partial_a.1), channel_id=1, source_target_pairs={{0,1},{1,0},{2,3},{3,2},{4,5},{5,4},{6,7},{7,6},{8,24},{9,25},{10,... | collective-permute-start | bytes 884744 | tf_op jit(solution)/shard_map/ppermute | solution.py:222
  33.3 7.9 %collective-permute-start.4 = (bf16[128,1152]{1,0:T(8,128)(2,1)S(1)}, bf16[128,1152]{1,0:T(8,128)(2,1)S(1)}, u32[]{:S(2)}, u32[]{:S(2)}) collective-permute-start(bf16[128,1152]{1,0:T(8,128)(2,1)S(1)} %partial_b.1), channel_id=1, source_target_pairs={{0,16},{1,17},{2,18},{3,19},{4,20},{5,21},{6,22},{7,23},{8,9},{9,8... | collective-permute-start | bytes 884744 | tf_op jit(solution)/shard_map/ppermute | solution.py:226

commit v4 on v3

--- a/solution.py
+++ b/solution.py
@@ -73,8 +73,7 @@
         b_ref[at] = unit(raw_ref[at])[0].astype(b_ref.dtype)
 
 
-def keep_kernel(a2_in, b2_in, a2_out, b2_out):
-    b2_out[...] = b2_in[...]
+def keep_kernel(a2_in, a2_out):
     a2_out[...] = a2_in[...]
 
 
@@ -112,19 +111,30 @@
         out_ref[:, at] = total.astype(out_ref.dtype)
 
 
-def contribute(pair_ref, q_ref, keys, out_ref):
-    coef = weigh(q_ref[...], joined(keys), *scalars_of(pair_ref))
-    collect(coef, keys, out_ref)
-
-
-def partial_a(pair_ref, pack_ref, other_ref, b2_ref, out_ref):
-    keys = (pack_ref.at[2], other_ref.at[0], other_ref.at[1], b2_ref)
-    contribute(pair_ref, pack_ref.at[1], keys, out_ref)
-
-
-def partial_b(pair_ref, pack_ref, other_ref, b2_ref, a2_ref, out_ref):
-    keys = (pack_ref.at[0], pack_ref.at[1], other_ref.at[2], a2_ref)
-    contribute(pair_ref, b2_ref, keys, out_ref)
+def contribute(pair_ref, jobs):
+    scale, shift = scalars_of(pair_ref)
+    coefs = [weigh(q[...], joined(keys), scale, shift) for q, keys, _, _ in jobs]
+    for coef, (_, keys, more, out_ref) in zip(coefs, jobs):
+        total = jnp.dot(coef, joined(keys), preferred_element_type=jnp.float32)
+        if more is not None:
+            total = total + more[...]
+        out_ref[...] = total.astype(out_ref.dtype)
+
+
+def early_kernel(pair_ref, pack_ref, b2_ref, half_a, half_b):
+    jobs = (
+        (pack_ref.at[1], (pack_ref.at[2], b2_ref), None, half_a),
+        (b2_ref, (pack_ref.at[0], pack_ref.at[1]), None, half_b),
+    )
+    contribute(pair_ref, jobs)
+
+
+def late_kernel(pair_ref, pack_ref, other_ref, b2_ref, a2_ref, half_a, half_b, out_a, out_b):
+    jobs = (
+        (pack_ref.at[1], (other_ref.at[0], other_ref.at[1]), half_a, out_a),
+        (b2_ref, (other_ref.at[2], a2_ref), half_b, out_b),
+    )
+    contribute(pair_ref, jobs)
 
 
 def norm_kernel(raw_a, raw_b, an_ref, bn_ref, ia_ref, ib_ref):
@@ -212,17 +222,19 @@
         pack_kernel, out_shape=pack, in_specs=[HERE] * 3, out_specs=HERE, name="pack"
     )(a, a1, b)
     other = lax.ppermute(mine, AXES, core_route)
-    a2, b2 = call(
-        keep_kernel, out_shape=(half, half), in_specs=[HERE] * 2, out_specs=(HERE, HERE),
-        name="keep", cost_estimate=LONG,
-    )(a2, b2)
-    part_a = call(
-        partial_a, out_shape=half, in_specs=[HERE] * 4, out_specs=HERE, name="partial_a"
-    )(pair, mine, other, b2)
+    half_a, half_b = call(
+        early_kernel, out_shape=(wide, wide), in_specs=[HERE] * 3, out_specs=(HERE, HERE),
+        name="early",
+    )(pair, mine, b2)
+    a2 = call(
+        keep_kernel, out_shape=half, in_specs=[HERE], out_specs=HERE, name="keep",
+        cost_estimate=LONG,
+    )(a2)
+    part_a, part_b = call(
+        late_kernel, out_shape=(half, half), in_specs=[HERE] * 7, out_specs=(HERE, HERE),
+        name="late",
+    )(pair, mine, other, b2, a2, half_a, half_b)
     back_a = lax.ppermute(part_a, AXES, first_route)
-    part_b = call(
-        partial_b, out_shape=half, in_specs=[HERE] * 5, out_specs=HERE, name="partial_b"
-    )(pair, mine, other, b2, a2)
     back_b = lax.ppermute(part_b, AXES, second_route)
     an, bn, ia, ib = call(
         norm_kernel, out_shape=(wide, wide, lanes, lanes), in_specs=[HERE] * 2,

time: 42.6 us -> 42.4 us (level)
    ppermute x1, waiting for transfers between devices: 1.25 us -> 0.35 us  [on_device(): a2 = lax.ppermute(b, AXES, crossed_route)]
    ppermute x1, waiting for transfers between devices: 1.25 us -> 1.94 us  [on_device(): back_b = lax.ppermute(part_b, AXES, second_route)]
where the time goes in v4:
time: 42.4 us; the launch traced here: 42.1 us
  starting transfers between devices  30 us (71%)
  Pallas kernels  7.69 us (18%)
  waiting for transfers between devices  2.3 us (5%)
  between operations  2.07 us (5%)
    ppermute x1, starting transfers between devices, on_device(): a2 = lax.ppermute(b, AXES, crossed_route)  13.9 us
    ppermute x1, starting transfers between devices, on_device(): a1 = lax.ppermute(a, AXES, first_route)  4.38 us
    ppermute x1, starting transfers between devices, on_device(): back_b = lax.ppermute(part_b, AXES, second_route)  3.21 us
    ppermute x1, starting transfers between devices, on_device(): b2 = lax.ppermute(b, AXES, second_route)  3.2 us
    ppermute x1, starting transfers between devices, on_device(): other = lax.ppermute(mine, AXES, core_route)  2.97 us
    ppermute x1, starting transfers between devices, on_device(): back_a = lax.ppermute(part_a, AXES, first_route)  2.37 us
    pallas_call x1, Pallas kernels, on_device(): call(own_kernel, out_shape=(wide, wide), in_specs=[HERE, AFAR] + [HERE] *...  2.2 us
    ppermute x1, waiting for transfers between devices, on_device(): back_b = lax.ppermute(part_b, AXES, second_route)  1.94 us
  transfers between devices with their start and end apart: 6, of which 2 were waited for; matrix products, arithmetic and copies ran while one was open for 0% of the time, Pallas kernels for 11%

profile of v4, /device:TPU:1, one launch (start us, length us, event | category | flops | bytes accessed | tf_op | source)
XLA Modules:
  0.0 42.1 jit_solution(3892340485403935752)
XLA Ops:
  0.6 1.2 %normalize_a.1 = (bf16[128,1152]{1,0:T(8,128)(2,1)S(1)}, bf16[128,1152]{1,0:T(8,128)(2,1)S(1)}, bf16[128,1152]{1,0:T(8,128)(2,1)S(1)}) custom-call(bf16[1,128,1152]{2,1,0:T(8,128)(2,1)} %x_ref.1, bf16[1,128,1152]{2,1,0:T(8,128)(2,1)} %y_ref.1), custom_call_target="tpu_custom_call" | custom-call | flops 1 | bytes 1 | tf_op jit(solution)/shard_map/normalize_a/pallas_call | solution.py:211
  1.9 4.4 %collective-permute-start = (bf16[128,1152]{1,0:T(8,128)(2,1)S(1)}, bf16[128,1152]{1,0:T(8,128)(2,1)S(1)}, u32[]{:S(2)}, u32[]{:S(2)}) collective-permute-start(bf16[128,1152]{1,0:T(8,128)(2,1)S(1)} %get-tuple-element.17.a_ref), channel_id=1, source_target_pairs={{0,1},{1,0},{2,3},{3,2},{4,5},{5,4},{6,7},{7,6},{8,24},{9,25},{10,... | collective-permute-start | bytes 884744 | tf_op jit(solution)/shard_map/ppermute | solution.py:215
  6.2 0.1 normalize_b.1.b_ref
  6.4 3.2 %collective-permute-start.2 = (bf16[128,1152]{1,0:T(8,128)(2,1)S(1)}, bf16[128,1152]{1,0:T(8,128)(2,1)S(1)}, u32[]{:S(2)}, u32[]{:S(2)}) collective-permute-start(bf16[128,1152]{1,0:T(8,128)(2,1)S(1)} %normalize_b.1.b_ref), channel_id=1, source_target_pairs={{0,16},{1,17},{2,18},{3,19},{4,20},{5,21},{6,22},{7,23},{8,9},{9,8... | collective-permute-start | bytes 884744 | tf_op jit(solution)/shard_map/ppermute | solution.py:219
  9.6 13.9 %collective-permute-start.3 = (bf16[128,1152]{1,0:T(8,128)(2,1)S(1)}, bf16[128,1152]{1,0:T(8,128)(2,1)S(1)}, u32[]{:S(2)}, u32[]{:S(2)}) collective-permute-start(bf16[128,1152]{1,0:T(8,128)(2,1)S(1)} %normalize_b.1.b_ref), channel_id=1, source_target_pairs={{0,24},{1,25},{2,26},{3,27},{4,28},{5,29},{6,30},{7,31},{8,1},{9,0... | collective-permute-start | bytes 884744 | tf_op jit(solution)/shard_map/ppermute | solution.py:220
  23.5 0.0 collective-permute-done.a1_ref
  23.5 0.1 pack.1.pack_ref
  23.6 3.0 %collective-permute-start.1 = (bf16[3,128,1152]{2,1,0:T(8,128)(2,1)S(1)}, bf16[3,128,1152]{2,1,0:T(8,128)(2,1)S(1)}, u32[]{:S(2)}, u32[]{:S(2)}) collective-permute-start(bf16[3,128,1152]{2,1,0:T(8,128)(2,1)S(1)} %pack.1.pack_ref), channel_id=1, source_target_pairs={{0,8},{1,9},{2,10},{3,11},{4,12},{5,13},{6,14},{7,15},{8,0},{9,1},... | collective-permute-start | bytes 2654216 | tf_op jit(solution)/shard_map/ppermute | solution.py:224
  27.8 0.0 collective-permute-done.2.b2_ref
  27.8 0.1 stack.6.pair_ref
  27.9 0.8 %early.1 = (f32[128,1152]{1,0:T(8,128)S(1)}, f32[128,1152]{1,0:T(8,128)S(1)}) custom-call(f32[2,8,128]{2,1,0:T(8,128)S(1)} %stack.6.pair_ref, bf16[3,128,1152]{2,1,0:T(8,128)(2,1)S(1)} %pack.1.pack_ref, bf16[128,1152]{1,0:T(8,128)(2,1)S(1)} %collective-permute-done.2.b2_ref), custom_call_target="tpu_custom_call" | custom-call | flops 1 | bytes 1 | tf_op jit(solution)/shard_map/early/pallas_call | solution.py:225
  28.7 0.4 collective-permute-done.3.a2_in
  29.1 0.0 collective-permute-done.1.other_ref
  29.1 0.8 %late.1 = (bf16[128,1152]{1,0:T(8,128)(2,1)S(1)}, bf16[128,1152]{1,0:T(8,128)(2,1)S(1)}) custom-call(f32[2,8,128]{2,1,0:T(8,128)S(1)} %stack.6.pair_ref, bf16[3,128,1152]{2,1,0:T(8,128)(2,1)S(1)} %pack.1.pack_ref, bf16[3,128,1152]{2,1,0:T(8,128)(2,1)S(1)} %collective-permute-done.1.other_ref, bf16[128,1152]{1,0:T(8,128)(2,1)S(1)} %collective-permute-done.2.b2_ref, ...), custom_call_target="tpu_custom_call" | custom-call | flops 1 | bytes 1 | tf_op jit(solution)/shard_map/late/pallas_call | solution.py:233
  30.0 2.4 %collective-permute-start.5 = (bf16[128,1152]{1,0:T(8,128)(2,1)S(1)}, bf16[128,1152]{1,0:T(8,128)(2,1)S(1)}, u32[]{:S(2)}, u32[]{:S(2)}) collective-permute-start(bf16[128,1152]{1,0:T(8,128)(2,1)S(1)} %get-tuple-element.27), channel_id=1, source_target_pairs={{0,1},{1,0},{2,3},{3,2},{4,5},{5,4},{6,7},{7,6},{8,24},{9,25},{10,... | collective-permute-start | bytes 884744 | tf_op jit(solution)/shard_map/ppermute | solution.py:237
  32.4 3.2 %collective-permute-start.4 = (bf16[128,1152]{1,0:T(8,128)(2,1)S(1)}, bf16[128,1152]{1,0:T(8,128)(2,1)S(1)}, u32[]{:S(2)}, u32[]{:S(2)}) collective-permute-start(bf16[128,1152]{1,0:T(8,128)(2,1)S(1)} %get-tuple-element.22), channel_id=1, source_target_pairs={{0,16},{1,17},{2,18},{3,19},{4,20},{5,21},{6,22},{7,23},{8,9},{9,8... | collective-permute-start | bytes 884744 | tf_op jit(solution)/shard_map/ppermute | solution.py:238
  35.6 0.2 norms.1
  35.8 2.2 %own.1 = (f32[128,1152]{1,0:T(8,128)S(1)}, f32[128,1152]{1,0:T(8,128)S(1)}) custom-call(f32[2,8,128]{2,1,0:T(8,128)S(1)} %stack.6.pair_ref, s32[1,1,128]{2,1,0:T(1,128)} %slot_ref.1, bf16[3,128,1152]{2,1,0:T(8,128)(2,1)S(1)} %pack.1.pack_ref, bf16[3,128,1152]{2,1,0:T(8,128)(2,1)S(1)} %collective-permute-done.1.other_ref, ...), custom_call_target="tpu_custom_call" | custom-call | flops 1 | bytes 1 | tf_op jit(solution)/shard_map/own/pallas_call | solution.py:243
  38.0 0.0 collective-permute-done.5.back
  38.0 1.1 %project_a.1 = (f32[1,128,1152]{2,1,0:T(8,128)}, f32[1,128,1152]{2,1,0:T(8,128)}) custom-call(f32[128,1152]{1,0:T(8,128)S(1)} %get-tuple-element.26.g_ref, bf16[128,1152]{1,0:T(8,128)(2,1)S(1)} %collective-permute-done.5.back, f32[128,1152]{1,0:T(8,128)S(1)} %get-tuple-element.28.n_ref, f32[128,128]{1,0:T(8,128)S(1)} %get-tuple-element.29.i_ref), custom_call_target="tpu_custom_call" | custom-call | flops 1 | bytes 1 | tf_op jit(solution)/shard_map/project_a/pallas_call | solution.py:251
  39.1 1.9 %collective-permute-done.4.back = bf16[128,1152]{1,0:T(8,128)(2,1)S(1)} collective-permute-done((bf16[128,1152]{1,0:T(8,128)(2,1)S(1)}, bf16[128,1152]{1,0:T(8,128)(2,1)S(1)}, u32[]{:S(2)}, u32[]{:S(2)}) %collective-permute-start.4) | collective-permute-done | bytes 294944 | tf_op jit(solution)/shard_map/ppermute | solution.py:238
  41.0 1.1 %project_b.1 = (f32[1,128,1152]{2,1,0:T(8,128)}, f32[1,128,1152]{2,1,0:T(8,128)}) custom-call(f32[128,1152]{1,0:T(8,128)S(1)} %get-tuple-element.19.g_ref, bf16[128,1152]{1,0:T(8,128)(2,1)S(1)} %collective-permute-done.4.back, f32[128,1152]{1,0:T(8,128)S(1)} %get-tuple-element.24.n_ref, ...), custom_call_target="tpu_custom_call", output_to_operand_aliasing={{0}: (4, {}), {1}: (5, {})} | custom-call | flops 1 | bytes 1 | tf_op jit(solution)/shard_map/project_b/pallas_call | solution.py:255
  (2 shorter events, 0.0 us)
Async XLA Ops:
  1.9 21.6 %collective-permute-start = (bf16[128,1152]{1,0:T(8,128)(2,1)S(1)}, bf16[128,1152]{1,0:T(8,128)(2,1)S(1)}, u32[]{:S(2)}, u32[]{:S(2)}) collective-permute-start(bf16[128,1152]{1,0:T(8,128)(2,1)S(1)} %get-tuple-element.17.a_ref), channel_id=1, source_target_pairs={{0,1},{1,0},{2,3},{3,2},{4,5},{5,4},{6,7},{7,6},{8,24},{9,25},{10,... | collective-permute-start | bytes 884744 | tf_op jit(solution)/shard_map/ppermute | solution.py:215
  6.4 21.4 %collective-permute-start.2 = (bf16[128,1152]{1,0:T(8,128)(2,1)S(1)}, bf16[128,1152]{1,0:T(8,128)(2,1)S(1)}, u32[]{:S(2)}, u32[]{:S(2)}) collective-permute-start(bf16[128,1152]{1,0:T(8,128)(2,1)S(1)} %normalize_b.1.b_ref), channel_id=1, source_target_pairs={{0,16},{1,17},{2,18},{3,19},{4,20},{5,21},{6,22},{7,23},{8,9},{9,8... | collective-permute-start | bytes 884744 | tf_op jit(solution)/shard_map/ppermute | solution.py:219
  9.6 19.5 %collective-permute-start.3 = (bf16[128,1152]{1,0:T(8,128)(2,1)S(1)}, bf16[128,1152]{1,0:T(8,128)(2,1)S(1)}, u32[]{:S(2)}, u32[]{:S(2)}) collective-permute-start(bf16[128,1152]{1,0:T(8,128)(2,1)S(1)} %normalize_b.1.b_ref), channel_id=1, source_target_pairs={{0,24},{1,25},{2,26},{3,27},{4,28},{5,29},{6,30},{7,31},{8,1},{9,0... | collective-permute-start | bytes 884744 | tf_op jit(solution)/shard_map/ppermute | solution.py:220
  23.6 5.6 %collective-permute-start.1 = (bf16[3,128,1152]{2,1,0:T(8,128)(2,1)S(1)}, bf16[3,128,1152]{2,1,0:T(8,128)(2,1)S(1)}, u32[]{:S(2)}, u32[]{:S(2)}) collective-permute-start(bf16[3,128,1152]{2,1,0:T(8,128)(2,1)S(1)} %pack.1.pack_ref), channel_id=1, source_target_pairs={{0,8},{1,9},{2,10},{3,11},{4,12},{5,13},{6,14},{7,15},{8,0},{9,1},... | collective-permute-start | bytes 2654216 | tf_op jit(solution)/shard_map/ppermute | solution.py:224
  30.0 8.0 %collective-permute-start.5 = (bf16[128,1152]{1,0:T(8,128)(2,1)S(1)}, bf16[128,1152]{1,0:T(8,128)(2,1)S(1)}, u32[]{:S(2)}, u32[]{:S(2)}) collective-permute-start(bf16[128,1152]{1,0:T(8,128)(2,1)S(1)} %get-tuple-element.27), channel_id=1, source_target_pairs={{0,1},{1,0},{2,3},{3,2},{4,5},{5,4},{6,7},{7,6},{8,24},{9,25},{10,... | collective-permute-start | bytes 884744 | tf_op jit(solution)/shard_map/ppermute | solution.py:237
  32.4 8.7 %collective-permute-start.4 = (bf16[128,1152]{1,0:T(8,128)(2,1)S(1)}, bf16[128,1152]{1,0:T(8,128)(2,1)S(1)}, u32[]{:S(2)}, u32[]{:S(2)}) collective-permute-start(bf16[128,1152]{1,0:T(8,128)(2,1)S(1)} %get-tuple-element.22), channel_id=1, source_target_pairs={{0,16},{1,17},{2,18},{3,19},{4,20},{5,21},{6,22},{7,23},{8,9},{9,8... | collective-permute-start | bytes 884744 | tf_op jit(solution)/shard_map/ppermute | solution.py:238

commit v5 on v4

--- a/solution.py
+++ b/solution.py
@@ -11,7 +11,8 @@
 HERE = pl.BlockSpec(memory_space=pltpu.VMEM)
 AFAR = pl.BlockSpec(memory_space=pltpu.HBM)
 SHORT = pl.CostEstimate(flops=1, bytes_accessed=1, transcendentals=0)
-LONG = pl.CostEstimate(flops=8_000_000_000, bytes_accessed=1, transcendentals=0)
+LONG = pl.CostEstimate(flops=9_000_000_000, bytes_accessed=1, transcendentals=0)
+FILL = pl.CostEstimate(flops=1_000_000_000, bytes_accessed=1, transcendentals=0)
 PARAMS = pltpu.CompilerParams(vmem_limit_bytes=32 * 1024 * 1024)
 CHUNK = 128
 
@@ -73,10 +74,6 @@
         b_ref[at] = unit(raw_ref[at])[0].astype(b_ref.dtype)
 
 
-def keep_kernel(a2_in, a2_out):
-    a2_out[...] = a2_in[...]
-
-
 def pack_kernel(a_ref, a1_ref, b_ref, pack_ref):
     for k, ref in enumerate((a_ref, a1_ref, b_ref)):
         pack_ref[k] = ref[...]
@@ -121,7 +118,7 @@
         out_ref[...] = total.astype(out_ref.dtype)
 
 
-def early_kernel(pair_ref, pack_ref, b2_ref, half_a, half_b):
+def early_kernel(pair_ref, pack_ref, b2_ref, _, half_a, half_b):
     jobs = (
         (pack_ref.at[1], (pack_ref.at[2], b2_ref), None, half_a),
         (b2_ref, (pack_ref.at[0], pack_ref.at[1]), None, half_b),
@@ -129,12 +126,13 @@
     contribute(pair_ref, jobs)
 
 
-def late_kernel(pair_ref, pack_ref, other_ref, b2_ref, a2_ref, half_a, half_b, out_a, out_b):
-    jobs = (
-        (pack_ref.at[1], (other_ref.at[0], other_ref.at[1]), half_a, out_a),
-        (b2_ref, (other_ref.at[2], a2_ref), half_b, out_b),
-    )
-    contribute(pair_ref, jobs)
+def late_a(pair_ref, pack_ref, other_ref, half_a, out_a):
+    keys = (other_ref.at[0], other_ref.at[1])
+    contribute(pair_ref, ((pack_ref.at[1], keys, half_a, out_a),))
+
+
+def late_b(pair_ref, b2_ref, other_ref, a2_ref, half_b, out_b):
+    contribute(pair_ref, ((b2_ref, (other_ref.at[2], a2_ref), half_b, out_b),))
 
 
 def norm_kernel(raw_a, raw_b, an_ref, bn_ref, ia_ref, ib_ref):
@@ -222,24 +220,22 @@
         pack_kernel, out_shape=pack, in_specs=[HERE] * 3, out_specs=HERE, name="pack"
     )(a, a1, b)
     other = lax.ppermute(mine, AXES, core_route)
+    an, bn, ia, ib = call(
+        norm_kernel, out_shape=(wide, wide, lanes, lanes), in_specs=[HERE] * 2,
+        out_specs=(HERE,) * 4, name="norms", cost_estimate=FILL,
+    )(raw_a, raw_b)
     half_a, half_b = call(
-        early_kernel, out_shape=(wide, wide), in_specs=[HERE] * 3, out_specs=(HERE, HERE),
-        name="early",
-    )(pair, mine, b2)
-    a2 = call(
-        keep_kernel, out_shape=half, in_specs=[HERE], out_specs=HERE, name="keep",
-        cost_estimate=LONG,
-    )(a2)
-    part_a, part_b = call(
-        late_kernel, out_shape=(half, half), in_specs=[HERE] * 7, out_specs=(HERE, HERE),
-        name="late",
-    )(pair, mine, other, b2, a2, half_a, half_b)
+        early_kernel, out_shape=(wide, wide), in_specs=[HERE] * 4, out_specs=(HERE, HERE),
+        name="early", cost_estimate=LONG,
+    )(pair, mine, b2, ia)
+    part_a = call(
+        late_a, out_shape=half, in_specs=[HERE] * 4, out_specs=HERE, name="late_a"
+    )(pair, mine, other, half_a)
+    part_b = call(
+        late_b, out_shape=half, in_specs=[HERE] * 5, out_specs=HERE, name="late_b"
+    )(pair, b2, other, a2, half_b)
     back_a = lax.ppermute(part_a, AXES, first_route)
     back_b = lax.ppermute(part_b, AXES, second_route)
-    an, bn, ia, ib = call(
-        norm_kernel, out_shape=(wide, wide, lanes, lanes), in_specs=[HERE] * 2,
-        out_specs=(HERE,) * 4, name="norms",
-    )(raw_a, raw_b)
     ga, gb = call(
         own_kernel, out_shape=(wide, wide), in_specs=[HERE, AFAR] + [HERE] * 4,
         out_specs=(HERE,) * 2,

time: 42.4 us -> 42.5 us (level)
  starting transfers between devices: 30 us -> 29 us
  waiting for transfers between devices: 2.3 us -> 2.8 us
  Pallas kernels: 7.69 us -> 8.15 us
    ppermute x1, starting transfers between devices: 3.21 us -> 2.03 us  [on_device(): back_b = lax.ppermute(part_b, AXES, second_route)]
    ppermute x1, waiting for transfers between devices: 1.94 us -> 2.54 us  [on_device(): back_b = lax.ppermute(part_b, AXES, second_route)]
    pallas_call x3, Pallas kernels: 1.69 us -> 2.16 us  [the longest x1 0.82 us: on_device(): call(early_kernel, out_shape=(wide, wide), in_specs=[HERE] * 4, out_specs...]
  transfers between devices with their start and end apart: 6 -> 6, of which waited for: 2 -> 2; matrix products, arithmetic and copies ran while one was open for 0% -> 0% of each run, Pallas kernels for 11% -> 14%
where the time goes in v5:
time: 42.5 us; the launch traced here: 42.1 us
  starting transfers between devices  29 us (68%)
  Pallas kernels  8.15 us (19%)
  waiting for transfers between devices  2.8 us (7%)
  between operations  2.07 us (5%)
    ppermute x1, starting transfers between devices, on_device(): a2 = lax.ppermute(b, AXES, crossed_route)  13.9 us
    ppermute x1, starting transfers between devices, on_device(): a1 = lax.ppermute(a, AXES, first_route)  4.38 us
    ppermute x1, starting transfers between devices, on_device(): b2 = lax.ppermute(b, AXES, second_route)  3.2 us
    ppermute x1, starting transfers between devices, on_device(): other = lax.ppermute(mine, AXES, core_route)  2.97 us
    ppermute x1, starting transfers between devices, on_device(): back_a = lax.ppermute(part_a, AXES, first_route)  2.61 us
    ppermute x1, waiting for transfers between devices, on_device(): back_b = lax.ppermute(part_b, AXES, second_route)  2.54 us
    pallas_call x1, Pallas kernels, on_device(): call(own_kernel, out_shape=(wide, wide), in_specs=[HERE, AFAR] + [HERE] *...  2.17 us
    ppermute x1, starting transfers between devices, on_device(): back_b = lax.ppermute(part_b, AXES, second_route)  2.03 us
  transfers between devices with their start and end apart: 6, of which 2 were waited for; matrix products, arithmetic and copies ran while one was open for 0% of the time, Pallas kernels for 14%

profile of v5, /device:TPU:1, one launch (start us, length us, event | category | flops | bytes accessed | tf_op | source)
XLA Modules:
  0.0 42.1 jit_solution(7909058698991970261)
XLA Ops:
  0.6 1.2 %normalize_a.1 = (bf16[128,1152]{1,0:T(8,128)(2,1)S(1)}, bf16[128,1152]{1,0:T(8,128)(2,1)S(1)}, bf16[128,1152]{1,0:T(8,128)(2,1)S(1)}) custom-call(bf16[1,128,1152]{2,1,0:T(8,128)(2,1)} %x_ref.1, bf16[1,128,1152]{2,1,0:T(8,128)(2,1)} %y_ref.1), custom_call_target="tpu_custom_call" | custom-call | flops 1 | bytes 1 | tf_op jit(solution)/shard_map/normalize_a/pallas_call | solution.py:209
  1.9 4.4 %collective-permute-start = (bf16[128,1152]{1,0:T(8,128)(2,1)S(1)}, bf16[128,1152]{1,0:T(8,128)(2,1)S(1)}, u32[]{:S(2)}, u32[]{:S(2)}) collective-permute-start(bf16[128,1152]{1,0:T(8,128)(2,1)S(1)} %get-tuple-element.15.a_ref), channel_id=1, source_target_pairs={{0,1},{1,0},{2,3},{3,2},{4,5},{5,4},{6,7},{7,6},{8,24},{9,25},{10,... | collective-permute-start | bytes 884744 | tf_op jit(solution)/shard_map/ppermute | solution.py:213
  6.2 0.1 normalize_b.1.b_ref
  6.4 3.2 %collective-permute-start.2 = (bf16[128,1152]{1,0:T(8,128)(2,1)S(1)}, bf16[128,1152]{1,0:T(8,128)(2,1)S(1)}, u32[]{:S(2)}, u32[]{:S(2)}) collective-permute-start(bf16[128,1152]{1,0:T(8,128)(2,1)S(1)} %normalize_b.1.b_ref), channel_id=1, source_target_pairs={{0,16},{1,17},{2,18},{3,19},{4,20},{5,21},{6,22},{7,23},{8,9},{9,8... | collective-permute-start | bytes 884744 | tf_op jit(solution)/shard_map/ppermute | solution.py:217
  9.6 13.9 %collective-permute-start.3 = (bf16[128,1152]{1,0:T(8,128)(2,1)S(1)}, bf16[128,1152]{1,0:T(8,128)(2,1)S(1)}, u32[]{:S(2)}, u32[]{:S(2)}) collective-permute-start(bf16[128,1152]{1,0:T(8,128)(2,1)S(1)} %normalize_b.1.b_ref), channel_id=1, source_target_pairs={{0,24},{1,25},{2,26},{3,27},{4,28},{5,29},{6,30},{7,31},{8,1},{9,0... | collective-permute-start | bytes 884744 | tf_op jit(solution)/shard_map/ppermute | solution.py:218
  23.5 0.0 collective-permute-done.a1_ref
  23.5 0.1 pack.1.pack_ref
  23.6 3.0 %collective-permute-start.1 = (bf16[3,128,1152]{2,1,0:T(8,128)(2,1)S(1)}, bf16[3,128,1152]{2,1,0:T(8,128)(2,1)S(1)}, u32[]{:S(2)}, u32[]{:S(2)}) collective-permute-start(bf16[3,128,1152]{2,1,0:T(8,128)(2,1)S(1)} %pack.1.pack_ref), channel_id=1, source_target_pairs={{0,8},{1,9},{2,10},{3,11},{4,12},{5,13},{6,14},{7,15},{8,0},{9,1},... | collective-permute-start | bytes 2654216 | tf_op jit(solution)/shard_map/ppermute | solution.py:222
  26.5 0.2 norms.1
  28.0 0.0 collective-permute-done.2.b2_ref
  28.1 0.1 stack.6.pair_ref
  28.1 0.8 %early.1 = (f32[128,1152]{1,0:T(8,128)S(1)}, f32[128,1152]{1,0:T(8,128)S(1)}) custom-call(f32[2,8,128]{2,1,0:T(8,128)S(1)} %stack.6.pair_ref, bf16[3,128,1152]{2,1,0:T(8,128)(2,1)S(1)} %pack.1.pack_ref, bf16[128,1152]{1,0:T(8,128)(2,1)S(1)} %collective-permute-done.2.b2_ref, f32[128,128]{1,0:T(8,128)S(1)} %get-tuple-element.19._.i_ref), custom_call_target="tpu_custom_call" | custom-call | flops 8999999488 | bytes 1 | tf_op jit(solution)/shard_map/early/pallas_call | solution.py:227
  29.0 0.0 collective-permute-done.1.other_ref
  29.0 0.7 %late_a.1 = bf16[128,1152]{1,0:T(8,128)(2,1)S(1)} custom-call(f32[2,8,128]{2,1,0:T(8,128)S(1)} %stack.6.pair_ref, bf16[3,128,1152]{2,1,0:T(8,128)(2,1)S(1)} %pack.1.pack_ref, bf16[3,128,1152]{2,1,0:T(8,128)(2,1)S(1)} %collective-permute-done.1.other_ref, f32[128,1152]{1,0:T(8,128)S(1)} %get-tuple-element.24.half_a), custom_call_target="tpu_custom_call" | custom-call | flops 1 | bytes 1 | tf_op jit(solution)/shard_map/late_a/pallas_call | solution.py:231
  29.6 2.6 %collective-permute-start.5 = (bf16[128,1152]{1,0:T(8,128)(2,1)S(1)}, bf16[128,1152]{1,0:T(8,128)(2,1)S(1)}, u32[]{:S(2)}, u32[]{:S(2)}) collective-permute-start(bf16[128,1152]{1,0:T(8,128)(2,1)S(1)} %late_a.1), channel_id=1, source_target_pairs={{0,1},{1,0},{2,3},{3,2},{4,5},{5,4},{6,7},{7,6},{8,24},{9,25},{10,... | collective-permute-start | bytes 884744 | tf_op jit(solution)/shard_map/ppermute | solution.py:237
  32.3 0.0 collective-permute-done.3.a2_ref
  32.3 0.7 %late_b.1 = bf16[128,1152]{1,0:T(8,128)(2,1)S(1)} custom-call(f32[2,8,128]{2,1,0:T(8,128)S(1)} %stack.6.pair_ref, bf16[128,1152]{1,0:T(8,128)(2,1)S(1)} %collective-permute-done.2.b2_ref, bf16[3,128,1152]{2,1,0:T(8,128)(2,1)S(1)} %collective-permute-done.1.other_ref, bf16[128,1152]{1,0:T(8,128)(2,1)S(1)} %collective-permute-done.3.a2_ref, ...), custom_call_target="tpu_custom_call" | custom-call | flops 1 | bytes 1 | tf_op jit(solution)/shard_map/late_b/pallas_call | solution.py:234
  32.9 2.0 %collective-permute-start.4 = (bf16[128,1152]{1,0:T(8,128)(2,1)S(1)}, bf16[128,1152]{1,0:T(8,128)(2,1)S(1)}, u32[]{:S(2)}, u32[]{:S(2)}) collective-permute-start(bf16[128,1152]{1,0:T(8,128)(2,1)S(1)} %late_b.1), channel_id=1, source_target_pairs={{0,16},{1,17},{2,18},{3,19},{4,20},{5,21},{6,22},{7,23},{8,9},{9,8... | collective-permute-start | bytes 884744 | tf_op jit(solution)/shard_map/ppermute | solution.py:238
  35.0 2.2 %own.1 = (f32[128,1152]{1,0:T(8,128)S(1)}, f32[128,1152]{1,0:T(8,128)S(1)}) custom-call(f32[2,8,128]{2,1,0:T(8,128)S(1)} %stack.6.pair_ref, s32[1,1,128]{2,1,0:T(1,128)} %slot_ref.1, bf16[3,128,1152]{2,1,0:T(8,128)(2,1)S(1)} %pack.1.pack_ref, bf16[3,128,1152]{2,1,0:T(8,128)(2,1)S(1)} %collective-permute-done.1.other_ref, ...), custom_call_target="tpu_custom_call" | custom-call | flops 1 | bytes 1 | tf_op jit(solution)/shard_map/own/pallas_call | solution.py:239
  37.2 0.2 collective-permute-done.5.back
  37.4 1.1 %project_a.1 = (f32[1,128,1152]{2,1,0:T(8,128)}, f32[1,128,1152]{2,1,0:T(8,128)}) custom-call(f32[128,1152]{1,0:T(8,128)S(1)} %get-tuple-element.23.g_ref, bf16[128,1152]{1,0:T(8,128)(2,1)S(1)} %collective-permute-done.5.back, f32[128,1152]{1,0:T(8,128)S(1)} %get-tuple-element.25.n_ref, f32[128,128]{1,0:T(8,128)S(1)} %get-tuple-element.19._.i_ref), custom_call_target="tpu_custom_call" | custom-call | flops 1 | bytes 1 | tf_op jit(solution)/shard_map/project_a/pallas_call | solution.py:247
  38.5 2.5 %collective-permute-done.4.back = bf16[128,1152]{1,0:T(8,128)(2,1)S(1)} collective-permute-done((bf16[128,1152]{1,0:T(8,128)(2,1)S(1)}, bf16[128,1152]{1,0:T(8,128)(2,1)S(1)}, u32[]{:S(2)}, u32[]{:S(2)}) %collective-permute-start.4) | collective-permute-done | bytes 294944 | tf_op jit(solution)/shard_map/ppermute | solution.py:238
  41.0 1.1 %project_b.1 = (f32[1,128,1152]{2,1,0:T(8,128)}, f32[1,128,1152]{2,1,0:T(8,128)}) custom-call(f32[128,1152]{1,0:T(8,128)S(1)} %get-tuple-element.17.g_ref, bf16[128,1152]{1,0:T(8,128)(2,1)S(1)} %collective-permute-done.4.back, f32[128,1152]{1,0:T(8,128)S(1)} %get-tuple-element.21.n_ref, ...), custom_call_target="tpu_custom_call", output_to_operand_aliasing={{0}: (4, {}), {1}: (5, {})} | custom-call | flops 1 | bytes 1 | tf_op jit(solution)/shard_map/project_b/pallas_call | solution.py:251
  (1 shorter events, 0.0 us)
Async XLA Ops:
  1.9 21.6 %collective-permute-start = (bf16[128,1152]{1,0:T(8,128)(2,1)S(1)}, bf16[128,1152]{1,0:T(8,128)(2,1)S(1)}, u32[]{:S(2)}, u32[]{:S(2)}) collective-permute-start(bf16[128,1152]{1,0:T(8,128)(2,1)S(1)} %get-tuple-element.15.a_ref), channel_id=1, source_target_pairs={{0,1},{1,0},{2,3},{3,2},{4,5},{5,4},{6,7},{7,6},{8,24},{9,25},{10,... | collective-permute-start | bytes 884744 | tf_op jit(solution)/shard_map/ppermute | solution.py:213
  6.4 21.7 %collective-permute-start.2 = (bf16[128,1152]{1,0:T(8,128)(2,1)S(1)}, bf16[128,1152]{1,0:T(8,128)(2,1)S(1)}, u32[]{:S(2)}, u32[]{:S(2)}) collective-permute-start(bf16[128,1152]{1,0:T(8,128)(2,1)S(1)} %normalize_b.1.b_ref), channel_id=1, source_target_pairs={{0,16},{1,17},{2,18},{3,19},{4,20},{5,21},{6,22},{7,23},{8,9},{9,8... | collective-permute-start | bytes 884744 | tf_op jit(solution)/shard_map/ppermute | solution.py:217
  9.6 22.6 %collective-permute-start.3 = (bf16[128,1152]{1,0:T(8,128)(2,1)S(1)}, bf16[128,1152]{1,0:T(8,128)(2,1)S(1)}, u32[]{:S(2)}, u32[]{:S(2)}) collective-permute-start(bf16[128,1152]{1,0:T(8,128)(2,1)S(1)} %normalize_b.1.b_ref), channel_id=1, source_target_pairs={{0,24},{1,25},{2,26},{3,27},{4,28},{5,29},{6,30},{7,31},{8,1},{9,0... | collective-permute-start | bytes 884744 | tf_op jit(solution)/shard_map/ppermute | solution.py:218
  23.6 5.4 %collective-permute-start.1 = (bf16[3,128,1152]{2,1,0:T(8,128)(2,1)S(1)}, bf16[3,128,1152]{2,1,0:T(8,128)(2,1)S(1)}, u32[]{:S(2)}, u32[]{:S(2)}) collective-permute-start(bf16[3,128,1152]{2,1,0:T(8,128)(2,1)S(1)} %pack.1.pack_ref), channel_id=1, source_target_pairs={{0,8},{1,9},{2,10},{3,11},{4,12},{5,13},{6,14},{7,15},{8,0},{9,1},... | collective-permute-start | bytes 2654216 | tf_op jit(solution)/shard_map/ppermute | solution.py:222
  29.6 7.8 %collective-permute-start.5 = (bf16[128,1152]{1,0:T(8,128)(2,1)S(1)}, bf16[128,1152]{1,0:T(8,128)(2,1)S(1)}, u32[]{:S(2)}, u32[]{:S(2)}) collective-permute-start(bf16[128,1152]{1,0:T(8,128)(2,1)S(1)} %late_a.1), channel_id=1, source_target_pairs={{0,1},{1,0},{2,3},{3,2},{4,5},{5,4},{6,7},{7,6},{8,24},{9,25},{10,... | collective-permute-start | bytes 884744 | tf_op jit(solution)/shard_map/ppermute | solution.py:237
  32.9 8.1 %collective-permute-start.4 = (bf16[128,1152]{1,0:T(8,128)(2,1)S(1)}, bf16[128,1152]{1,0:T(8,128)(2,1)S(1)}, u32[]{:S(2)}, u32[]{:S(2)}) collective-permute-start(bf16[128,1152]{1,0:T(8,128)(2,1)S(1)} %late_b.1), channel_id=1, source_target_pairs={{0,16},{1,17},{2,18},{3,19},{4,20},{5,21},{6,22},{7,23},{8,9},{9,8... | collective-permute-start | bytes 884744 | tf_op jit(solution)/shard_map/ppermute | solution.py:238

commit v6 on v4

--- a/solution.py
+++ b/solution.py
@@ -25,15 +25,15 @@
             over_z = (d ^ 2) * n_group + g
             over_y = d * n_group + (g ^ 1)
             core.append((here, over_core))
-            first.append((here, over_z if d & 1 else over_y))
-            second.append((here, over_y if d & 1 else over_z))
+            first.append((here, over_y if d & 1 else over_z))
+            second.append((here, over_z if d & 1 else over_y))
             cross_y, cross_z = (d ^ 1) * n_group + (g ^ 1), (d ^ 3) * n_group + g
-            crossed.append((here, cross_y if d & 1 else cross_z))
+            crossed.append((here, cross_z if d & 1 else cross_y))
     return core, first, second, crossed
 
 
 def core_of():
-    return lax.axis_index("dp") & 1
+    return 1 - (lax.axis_index("dp") & 1)
 
 
 def load_chunks(x_ref, y_ref, swap, raw, sems):

time: 42.4 us -> 42.5 us (level)
  no operation moved by 1% of the time
where the time goes in v6:
time: 42.5 us; the launch traced here: 42.2 us
  starting transfers between devices  30.2 us (71%)
  Pallas kernels  7.58 us (18%)
  waiting for transfers between devices  2.31 us (5%)
  between operations  2.07 us (5%)
    ppermute x1, starting transfers between devices, on_device(): a2 = lax.ppermute(b, AXES, crossed_route)  14 us
    ppermute x1, starting transfers between devices, on_device(): a1 = lax.ppermute(a, AXES, first_route)  4.03 us
    ppermute x1, starting transfers between devices, on_device(): b2 = lax.ppermute(b, AXES, second_route)  3.55 us
    ppermute x1, starting transfers between devices, on_device(): back_b = lax.ppermute(part_b, AXES, second_route)  3.19 us
    ppermute x1, starting transfers between devices, on_device(): other = lax.ppermute(mine, AXES, core_route)  2.97 us
    ppermute x1, starting transfers between devices, on_device(): back_a = lax.ppermute(part_a, AXES, first_route)  2.39 us
    pallas_call x1, Pallas kernels, on_device(): call(own_kernel, out_shape=(wide, wide), in_specs=[HERE, AFAR] + [HERE] *...  2.19 us
    ppermute x1, waiting for transfers between devices, on_device(): back_b = lax.ppermute(part_b, AXES, second_route)  1.96 us
  transfers between devices with their start and end apart: 6, of which 2 were waited for; matrix products, arithmetic and copies ran while one was open for 0% of the time, Pallas kernels for 11%

profile of v6, /device:TPU:1, one launch (start us, length us, event | category | flops | bytes accessed | tf_op | source)
XLA Modules:
  0.0 42.2 jit_solution(648080051864290310)
XLA Ops:
  0.6 1.1 %normalize_a.1 = (bf16[128,1152]{1,0:T(8,128)(2,1)S(1)}, bf16[128,1152]{1,0:T(8,128)(2,1)S(1)}, bf16[128,1152]{1,0:T(8,128)(2,1)S(1)}) custom-call(bf16[1,128,1152]{2,1,0:T(8,128)(2,1)} %x_ref.1, bf16[1,128,1152]{2,1,0:T(8,128)(2,1)} %y_ref.1), custom_call_target="tpu_custom_call" | custom-call | flops 1 | bytes 1 | tf_op jit(solution)/shard_map/normalize_a/pallas_call | solution.py:211
  1.8 4.0 %collective-permute-start = (bf16[128,1152]{1,0:T(8,128)(2,1)S(1)}, bf16[128,1152]{1,0:T(8,128)(2,1)S(1)}, u32[]{:S(2)}, u32[]{:S(2)}) collective-permute-start(bf16[128,1152]{1,0:T(8,128)(2,1)S(1)} %get-tuple-element.17.a_ref), channel_id=1, source_target_pairs={{0,16},{1,17},{2,18},{3,19},{4,20},{5,21},{6,22},{7,23},{8,9},{9,8... | collective-permute-start | bytes 884744 | tf_op jit(solution)/shard_map/ppermute | solution.py:215
  5.8 0.1 normalize_b.1.b_ref
  6.0 3.5 %collective-permute-start.2 = (bf16[128,1152]{1,0:T(8,128)(2,1)S(1)}, bf16[128,1152]{1,0:T(8,128)(2,1)S(1)}, u32[]{:S(2)}, u32[]{:S(2)}) collective-permute-start(bf16[128,1152]{1,0:T(8,128)(2,1)S(1)} %normalize_b.1.b_ref), channel_id=1, source_target_pairs={{0,1},{1,0},{2,3},{3,2},{4,5},{5,4},{6,7},{7,6},{8,24},{9,25},{10,... | collective-permute-start | bytes 884744 | tf_op jit(solution)/shard_map/ppermute | solution.py:219
  9.5 14.0 %collective-permute-start.3 = (bf16[128,1152]{1,0:T(8,128)(2,1)S(1)}, bf16[128,1152]{1,0:T(8,128)(2,1)S(1)}, u32[]{:S(2)}, u32[]{:S(2)}) collective-permute-start(bf16[128,1152]{1,0:T(8,128)(2,1)S(1)} %normalize_b.1.b_ref), channel_id=1, source_target_pairs={{0,9},{1,8},{2,11},{3,10},{4,13},{5,12},{6,15},{7,14},{8,16},{9,17... | collective-permute-start | bytes 884744 | tf_op jit(solution)/shard_map/ppermute | solution.py:220
  23.6 0.0 collective-permute-done.a1_ref
  23.6 0.1 pack.1.pack_ref
  23.6 3.0 %collective-permute-start.1 = (bf16[3,128,1152]{2,1,0:T(8,128)(2,1)S(1)}, bf16[3,128,1152]{2,1,0:T(8,128)(2,1)S(1)}, u32[]{:S(2)}, u32[]{:S(2)}) collective-permute-start(bf16[3,128,1152]{2,1,0:T(8,128)(2,1)S(1)} %pack.1.pack_ref), channel_id=1, source_target_pairs={{0,8},{1,9},{2,10},{3,11},{4,12},{5,13},{6,14},{7,15},{8,0},{9,1},... | collective-permute-start | bytes 2654216 | tf_op jit(solution)/shard_map/ppermute | solution.py:224
  27.9 0.0 collective-permute-done.2.b2_ref
  27.9 0.1 stack.6.pair_ref
  28.0 0.8 %early.1 = (f32[128,1152]{1,0:T(8,128)S(1)}, f32[128,1152]{1,0:T(8,128)S(1)}) custom-call(f32[2,8,128]{2,1,0:T(8,128)S(1)} %stack.6.pair_ref, bf16[3,128,1152]{2,1,0:T(8,128)(2,1)S(1)} %pack.1.pack_ref, bf16[128,1152]{1,0:T(8,128)(2,1)S(1)} %collective-permute-done.2.b2_ref), custom_call_target="tpu_custom_call" | custom-call | flops 1 | bytes 1 | tf_op jit(solution)/shard_map/early/pallas_call | solution.py:225
  28.8 0.3 collective-permute-done.3.a2_in
  29.2 0.0 collective-permute-done.1.other_ref
  29.2 0.8 %late.1 = (bf16[128,1152]{1,0:T(8,128)(2,1)S(1)}, bf16[128,1152]{1,0:T(8,128)(2,1)S(1)}) custom-call(f32[2,8,128]{2,1,0:T(8,128)S(1)} %stack.6.pair_ref, bf16[3,128,1152]{2,1,0:T(8,128)(2,1)S(1)} %pack.1.pack_ref, bf16[3,128,1152]{2,1,0:T(8,128)(2,1)S(1)} %collective-permute-done.1.other_ref, bf16[128,1152]{1,0:T(8,128)(2,1)S(1)} %collective-permute-done.2.b2_ref, ...), custom_call_target="tpu_custom_call" | custom-call | flops 1 | bytes 1 | tf_op jit(solution)/shard_map/late/pallas_call | solution.py:233
  30.1 2.4 %collective-permute-start.5 = (bf16[128,1152]{1,0:T(8,128)(2,1)S(1)}, bf16[128,1152]{1,0:T(8,128)(2,1)S(1)}, u32[]{:S(2)}, u32[]{:S(2)}) collective-permute-start(bf16[128,1152]{1,0:T(8,128)(2,1)S(1)} %get-tuple-element.27), channel_id=1, source_target_pairs={{0,16},{1,17},{2,18},{3,19},{4,20},{5,21},{6,22},{7,23},{8,9},{9,8... | collective-permute-start | bytes 884744 | tf_op jit(solution)/shard_map/ppermute | solution.py:237
  32.5 3.2 %collective-permute-start.4 = (bf16[128,1152]{1,0:T(8,128)(2,1)S(1)}, bf16[128,1152]{1,0:T(8,128)(2,1)S(1)}, u32[]{:S(2)}, u32[]{:S(2)}) collective-permute-start(bf16[128,1152]{1,0:T(8,128)(2,1)S(1)} %get-tuple-element.22), channel_id=1, source_target_pairs={{0,1},{1,0},{2,3},{3,2},{4,5},{5,4},{6,7},{7,6},{8,24},{9,25},{10,... | collective-permute-start | bytes 884744 | tf_op jit(solution)/shard_map/ppermute | solution.py:238
  35.6 0.2 norms.1
  35.9 2.2 %own.1 = (f32[128,1152]{1,0:T(8,128)S(1)}, f32[128,1152]{1,0:T(8,128)S(1)}) custom-call(f32[2,8,128]{2,1,0:T(8,128)S(1)} %stack.6.pair_ref, s32[1,1,128]{2,1,0:T(1,128)} %slot_ref.1, bf16[3,128,1152]{2,1,0:T(8,128)(2,1)S(1)} %pack.1.pack_ref, bf16[3,128,1152]{2,1,0:T(8,128)(2,1)S(1)} %collective-permute-done.1.other_ref, ...), custom_call_target="tpu_custom_call" | custom-call | flops 1 | bytes 1 | tf_op jit(solution)/shard_map/own/pallas_call | solution.py:243
  38.1 0.0 collective-permute-done.5.back
  38.1 1.1 %project_a.1 = (f32[1,128,1152]{2,1,0:T(8,128)}, f32[1,128,1152]{2,1,0:T(8,128)}) custom-call(f32[128,1152]{1,0:T(8,128)S(1)} %get-tuple-element.26.g_ref, bf16[128,1152]{1,0:T(8,128)(2,1)S(1)} %collective-permute-done.5.back, f32[128,1152]{1,0:T(8,128)S(1)} %get-tuple-element.28.n_ref, f32[128,128]{1,0:T(8,128)S(1)} %get-tuple-element.29.i_ref), custom_call_target="tpu_custom_call" | custom-call | flops 1 | bytes 1 | tf_op jit(solution)/shard_map/project_a/pallas_call | solution.py:251
  39.1 2.0 %collective-permute-done.4.back = bf16[128,1152]{1,0:T(8,128)(2,1)S(1)} collective-permute-done((bf16[128,1152]{1,0:T(8,128)(2,1)S(1)}, bf16[128,1152]{1,0:T(8,128)(2,1)S(1)}, u32[]{:S(2)}, u32[]{:S(2)}) %collective-permute-start.4) | collective-permute-done | bytes 294944 | tf_op jit(solution)/shard_map/ppermute | solution.py:238
  41.1 1.1 %project_b.1 = (f32[1,128,1152]{2,1,0:T(8,128)}, f32[1,128,1152]{2,1,0:T(8,128)}) custom-call(f32[128,1152]{1,0:T(8,128)S(1)} %get-tuple-element.19.g_ref, bf16[128,1152]{1,0:T(8,128)(2,1)S(1)} %collective-permute-done.4.back, f32[128,1152]{1,0:T(8,128)S(1)} %get-tuple-element.24.n_ref, ...), custom_call_target="tpu_custom_call", output_to_operand_aliasing={{0}: (4, {}), {1}: (5, {})} | custom-call | flops 1 | bytes 1 | tf_op jit(solution)/shard_map/project_b/pallas_call | solution.py:255
  (2 shorter events, 0.0 us)
Async XLA Ops:
  1.8 21.8 %collective-permute-start = (bf16[128,1152]{1,0:T(8,128)(2,1)S(1)}, bf16[128,1152]{1,0:T(8,128)(2,1)S(1)}, u32[]{:S(2)}, u32[]{:S(2)}) collective-permute-start(bf16[128,1152]{1,0:T(8,128)(2,1)S(1)} %get-tuple-element.17.a_ref), channel_id=1, source_target_pairs={{0,16},{1,17},{2,18},{3,19},{4,20},{5,21},{6,22},{7,23},{8,9},{9,8... | collective-permute-start | bytes 884744 | tf_op jit(solution)/shard_map/ppermute | solution.py:215
  6.0 22.0 %collective-permute-start.2 = (bf16[128,1152]{1,0:T(8,128)(2,1)S(1)}, bf16[128,1152]{1,0:T(8,128)(2,1)S(1)}, u32[]{:S(2)}, u32[]{:S(2)}) collective-permute-start(bf16[128,1152]{1,0:T(8,128)(2,1)S(1)} %normalize_b.1.b_ref), channel_id=1, source_target_pairs={{0,1},{1,0},{2,3},{3,2},{4,5},{5,4},{6,7},{7,6},{8,24},{9,25},{10,... | collective-permute-start | bytes 884744 | tf_op jit(solution)/shard_map/ppermute | solution.py:219
  9.5 19.7 %collective-permute-start.3 = (bf16[128,1152]{1,0:T(8,128)(2,1)S(1)}, bf16[128,1152]{1,0:T(8,128)(2,1)S(1)}, u32[]{:S(2)}, u32[]{:S(2)}) collective-permute-start(bf16[128,1152]{1,0:T(8,128)(2,1)S(1)} %normalize_b.1.b_ref), channel_id=1, source_target_pairs={{0,9},{1,8},{2,11},{3,10},{4,13},{5,12},{6,15},{7,14},{8,16},{9,17... | collective-permute-start | bytes 884744 | tf_op jit(solution)/shard_map/ppermute | solution.py:220
  23.6 5.6 %collective-permute-start.1 = (bf16[3,128,1152]{2,1,0:T(8,128)(2,1)S(1)}, bf16[3,128,1152]{2,1,0:T(8,128)(2,1)S(1)}, u32[]{:S(2)}, u32[]{:S(2)}) collective-permute-start(bf16[3,128,1152]{2,1,0:T(8,128)(2,1)S(1)} %pack.1.pack_ref), channel_id=1, source_target_pairs={{0,8},{1,9},{2,10},{3,11},{4,12},{5,13},{6,14},{7,15},{8,0},{9,1},... | collective-permute-start | bytes 2654216 | tf_op jit(solution)/shard_map/ppermute | solution.py:224
  30.1 8.0 %collective-permute-start.5 = (bf16[128,1152]{1,0:T(8,128)(2,1)S(1)}, bf16[128,1152]{1,0:T(8,128)(2,1)S(1)}, u32[]{:S(2)}, u32[]{:S(2)}) collective-permute-start(bf16[128,1152]{1,0:T(8,128)(2,1)S(1)} %get-tuple-element.27), channel_id=1, source_target_pairs={{0,16},{1,17},{2,18},{3,19},{4,20},{5,21},{6,22},{7,23},{8,9},{9,8... | collective-permute-start | bytes 884744 | tf_op jit(solution)/shard_map/ppermute | solution.py:237
  32.5 8.6 %collective-permute-start.4 = (bf16[128,1152]{1,0:T(8,128)(2,1)S(1)}, bf16[128,1152]{1,0:T(8,128)(2,1)S(1)}, u32[]{:S(2)}, u32[]{:S(2)}) collective-permute-start(bf16[128,1152]{1,0:T(8,128)(2,1)S(1)} %get-tuple-element.22), channel_id=1, source_target_pairs={{0,1},{1,0},{2,3},{3,2},{4,5},{5,4},{6,7},{7,6},{8,24},{9,25},{10,... | collective-permute-start | bytes 884744 | tf_op jit(solution)/shard_map/ppermute | solution.py:238
